TPU v7x, 128 devices: a whole 4x4x4 slice. The times are simulated.
128 devices in a mesh: rep: 16 (over z, x_lo, core), tp: 8 (over y, x_hi).
Axes of the slice: x: 4 (x_hi: 2, x_lo: 2; x = x_hi * 2 + x_lo), y: 4, z: 4, core: 2. Of those that a mesh axis runs over, the one named last changes fastest.
Arguments:
- tokens_x: bfloat16 [512, 2, 8192], P('tp', None, 'rep'), may hold values from -6 to 6
- slot_rows: int32 [512], replicated, may hold values from 0 to 511, each once
- cache_keys: bfloat16 [512, 8, 384, 128], P('rep', 'tp'), may hold values from -460 to 460
- cache_values: bfloat16 [512, 8, 384, 128], P('rep', 'tp'), may hold values from -48 to 48
- lengths: int32 [512], P('rep'), may hold values from 2 to 384, as said below
- master_query: float32 [8192, 4096], P('rep', 'tp'), may hold values from -0.0625 to 0.0625
- moment_query: float32 [8192, 4096], P('rep', 'tp'), may hold values from -6 to 6
- second_query: float32 [8192, 4096], P('rep', 'tp'), may hold values from 0.1 to 10
- gradient_query: bfloat16 [8192, 4096], P('rep', 'tp'), may hold values from -6 to 6
- master_keyval: float32 [8192, 2, 1024], P('rep', None, 'tp'), may hold values from -0.0625 to 0.0625
- moment_keyval: float32 [8192, 2, 1024], P('rep', None, 'tp'), may hold values from -6 to 6
- second_keyval: float32 [8192, 2, 1024], P('rep', None, 'tp'), may hold values from 0.1 to 10
- gradient_keyval: bfloat16 [8192, 2, 1024], P('rep', None, 'tp'), may hold values from -6 to 6
- master_output: float32 [4096, 8192], P('tp', 'rep'), may hold values from -0.375 to 0.375
- moment_output: float32 [4096, 8192], P('tp', 'rep'), may hold values from -6 to 6
- second_output: float32 [4096, 8192], P('tp', 'rep'), may hold values from 0.1 to 10
- gradient_output: bfloat16 [4096, 8192], P('tp', 'rep'), may hold values from -6 to 6
Outputs:
- new_master_query: float32 [8192, 4096], P('rep', 'tp')
- new_moment_query: float32 [8192, 4096], P('rep', 'tp')
- new_second_query: float32 [8192, 4096], P('rep', 'tp')
- new_master_keyval: float32 [8192, 2, 1024], P('rep', None, 'tp')
- new_moment_keyval: float32 [8192, 2, 1024], P('rep', None, 'tp')
- new_second_keyval: float32 [8192, 2, 1024], P('rep', None, 'tp')
- new_master_output: float32 [4096, 8192], P('tp', 'rep')
- new_moment_output: float32 [4096, 8192], P('tp', 'rep')
- new_second_output: float32 [4096, 8192], P('tp', 'rep')
- decoded: bfloat16 [512, 2, 8192], P('rep', None, 'tp')
Inputs may be any that keep to these rules, and one draw needn't show every extreme that they name: `slot_rows`: a permutation of the rows. `lengths`: some slot has exactly 384.
All inputs are finite; a program needn't handle non-finite values.
Results may differ from a plain program's by a relative error of at most 0.017.
Values may be sent and summed in bfloat16 or wider, within the bound.
No kernel may reach another device: no remote copies, remote signals or barrier semaphores. Data moves between devices by JAX's collectives and lax.ppermute only.
A program may use at most 320 MiB of HBM per device.

v0:
```python
import jax
import jax.numpy as jnp
from jax import lax
from jax.sharding import PartitionSpec as P

learn_rate = 0.002
beta_one = 0.9
beta_two = 0.95
adam_eps = 1e-08
weight_decay = 0.1
step_count = 100.0
rope_base = 500000.0


def adam_step(master, moment, second, gradient):
    grad_wide = gradient.astype(jnp.float32)
    new_moment = beta_one * moment + (1.0 - beta_one) * grad_wide
    new_second = beta_two * second + (1.0 - beta_two) * grad_wide * grad_wide
    moment_hat = new_moment / (1.0 - beta_one**step_count)
    second_hat = new_second / (1.0 - beta_two**step_count)
    new_master = master - learn_rate * (
        moment_hat / (jnp.sqrt(second_hat) + adam_eps) + weight_decay * master
    )
    return (new_master, new_moment, new_second)


def rotate(vectors, positions):
    head_size = vectors.shape[-1]
    half = head_size // 2
    freqs = rope_base ** (-2.0 * jnp.arange(half, dtype=jnp.float32) / head_size)
    angles = positions[:, :, None, None].astype(jnp.float32) * freqs
    cosine = jnp.cos(angles)
    sine = jnp.sin(angles)
    first = vectors[..., :half]
    latter = vectors[..., half:]
    return jnp.concatenate(
        [first * cosine - latter * sine, latter * cosine + first * sine], axis=-1
    )


def attend(q_rot, k_new, v_new, keys, values, lengths):
    rows, steps, heads, head_size = q_rot.shape
    key_heads = keys.shape[1]
    group = heads // key_heads
    cache = keys.shape[2]
    q_five = q_rot.reshape(rows, steps, key_heads, group, head_size)
    scale = 1.0 / head_size**0.5
    old_scores = (
        jnp.einsum("rskgd,rkcd->rskgc", q_five, keys, preferred_element_type=jnp.float32) * scale
    )
    new_scores = (
        jnp.einsum("rskgd,rjkd->rskgj", q_five, k_new, preferred_element_type=jnp.float32) * scale
    )
    valid = jnp.arange(cache, dtype=jnp.int32)[None, :] < lengths[:, None]
    old_scores = jnp.where(valid[:, None, None, None, :], old_scores, -1e30)
    causal = (
        jnp.arange(steps, dtype=jnp.int32)[None, :] <= jnp.arange(steps, dtype=jnp.int32)[:, None]
    )
    new_scores = jnp.where(causal[None, :, None, None, :], new_scores, -1e30)
    top = jnp.maximum(
        jnp.max(old_scores, axis=-1, keepdims=True), jnp.max(new_scores, axis=-1, keepdims=True)
    )
    exp_old = jnp.exp(old_scores - top)
    exp_new = jnp.exp(new_scores - top)
    total = jnp.sum(exp_old, axis=-1, keepdims=True) + jnp.sum(exp_new, axis=-1, keepdims=True)
    weight_old = (exp_old / total).astype(jnp.bfloat16)
    weight_new = (exp_new / total).astype(jnp.bfloat16)
    mixed = jnp.einsum("rskgc,rkcd->rskgd", weight_old, values, preferred_element_type=jnp.float32)
    mixed = mixed + jnp.einsum(
        "rskgj,rjkd->rskgd", weight_new, v_new, preferred_element_type=jnp.float32
    )
    return mixed.reshape(rows, steps, heads * head_size).astype(jnp.bfloat16)


def per_device(
    tokens_x,
    slot_rows,
    cache_keys,
    cache_values,
    lengths,
    master_query,
    moment_query,
    second_query,
    gradient_query,
    master_keyval,
    moment_keyval,
    second_keyval,
    gradient_keyval,
    master_output,
    moment_output,
    second_output,
    gradient_output,
):
    state_query = adam_step(master_query, moment_query, second_query, gradient_query)
    state_keyval = adam_step(master_keyval, moment_keyval, second_keyval, gradient_keyval)
    state_output = adam_step(master_output, moment_output, second_output, gradient_output)
    w_query = state_query[0].astype(jnp.bfloat16)
    w_keyval = state_keyval[0].astype(jnp.bfloat16).reshape(master_keyval.shape[0], -1)
    w_output = state_output[0].astype(jnp.bfloat16)
    rows_rep = cache_keys.shape[0]
    steps = tokens_x.shape[1]
    head_size = cache_keys.shape[3]
    key_heads = cache_keys.shape[1]
    query_cols = w_query.shape[1]
    gathered = lax.all_gather(tokens_x, "tp", axis=0, tiled=True)
    ordered = jnp.take(gathered, slot_rows, axis=0)
    local_rows = lax.all_to_all(ordered, "rep", split_axis=0, concat_axis=2, tiled=True)
    flat_rows = local_rows.reshape(rows_rep * steps, -1)
    query = jnp.dot(
        flat_rows,
        lax.all_gather(w_query, "rep", axis=0, tiled=True),
        preferred_element_type=jnp.float32,
    )
    keyval = jnp.dot(
        flat_rows,
        lax.all_gather(w_keyval, "rep", axis=0, tiled=True),
        preferred_element_type=jnp.float32,
    )
    query = query.reshape(rows_rep, steps, query_cols // head_size, head_size)
    keyval = keyval.reshape(rows_rep, steps, 2, key_heads, head_size)
    positions = lengths[:, None] + jnp.arange(steps, dtype=jnp.int32)[None, :]
    q_rot = rotate(query, positions).astype(jnp.bfloat16)
    k_new = rotate(keyval[:, :, 0], positions).astype(jnp.bfloat16)
    v_new = keyval[:, :, 1].astype(jnp.bfloat16)
    attended = attend(q_rot, k_new, v_new, cache_keys, cache_values, lengths).reshape(
        rows_rep * steps, query_cols
    )
    partial_out = jnp.dot(
        attended,
        lax.all_gather(w_output, "rep", axis=1, tiled=True),
        preferred_element_type=jnp.float32,
    )
    partial_out = partial_out.reshape(rows_rep, steps, -1)
    decoded = lax.psum_scatter(
        partial_out.astype(jnp.bfloat16), "tp", scatter_dimension=2, tiled=True
    )
    return (
        state_query[0],
        state_query[1],
        state_query[2],
        state_keyval[0],
        state_keyval[1],
        state_keyval[2],
        state_output[0],
        state_output[1],
        state_output[2],
        decoded,
    )


def solution(mesh):
    return jax.shard_map(
        per_device,
        mesh=mesh,
        in_specs=(
            P("tp", None, "rep"),
            P(),
            P("rep", "tp", None, None),
            P("rep", "tp", None, None),
            P("rep"),
            P("rep", "tp"),
            P("rep", "tp"),
            P("rep", "tp"),
            P("rep", "tp"),
            P("rep", None, "tp"),
            P("rep", None, "tp"),
            P("rep", None, "tp"),
            P("rep", None, "tp"),
            P("tp", "rep"),
            P("tp", "rep"),
            P("tp", "rep"),
            P("tp", "rep"),
        ),
        out_specs=(
            P("rep", "tp"),
            P("rep", "tp"),
            P("rep", "tp"),
            P("rep", None, "tp"),
            P("rep", None, "tp"),
            P("rep", None, "tp"),
            P("tp", "rep"),
            P("tp", "rep"),
            P("tp", "rep"),
            P("rep", None, "tp"),
        ),
        check_vma=False,
    )
```

profile of v0, /device:TPU:24, one launch (start us, length us, event | category | flops | bytes accessed | tf_op | source)
XLA Modules:
  0.0 302.6 jit_solution(9229251038344391446)
XLA Ops:
  7.2 0.7 all-gather.5.cloned.1.call-update
  8.0 4.5 %fusion.63 = (bf16[512,2,128]{2,1,0:T(2,128)(2,1)S(1)}, f32[512,2,128]{2,1,0:T(2,128)}, f32[512,2,128]{2,1,0:T(2,128)}, f32[512,2,128]{2,1,0:T(2,128)}) fusion(f32[512,2,128]{2,1,0:T(2,128)} %param.26, bf16[512,2,128]{2,1,0:T(2,128)(2,1)} %param.29, f32[512,2,128]{2,1,0:T(2,128)} %param.27, f32[512,2,128]{2,1,0:T(2,128)} %param.28), kind=kLoop, calls=%fused_computation.83 | loop fusion | flops 2228224 | bytes 3670016 | tf_op jit(solution)/shard_map/convert_element_type | solution.py:98
  12.5 0.9 copy.50
  13.5 4.4 %fusion.66 = (bf16[512,512]{1,0:T(8,128)(2,1)}, f32[512,512]{1,0:T(8,128)}, f32[512,512]{1,0:T(8,128)}, f32[512,512]{1,0:T(8,128)}) fusion(f32[512,512]{1,0:T(8,128)} %param.22, bf16[512,512]{1,0:T(8,128)(2,1)} %param.25, f32[512,512]{1,0:T(8,128)} %param.23, f32[512,512]{1,0:T(8,128)} %param.24), kind=kLoop, calls=%fused_computation.84 | loop fusion | flops 4456448 | bytes 7340032 | tf_op jit(solution)/shard_map/convert_element_type | solution.py:97
  18.0 4.4 %fusion.69 = (bf16[512,512]{1,0:T(8,128)(2,1)}, f32[512,512]{1,0:T(8,128)}, f32[512,512]{1,0:T(8,128)}, f32[512,512]{1,0:T(8,128)}) fusion(f32[512,512]{1,0:T(8,128)} %param.30, bf16[512,512]{1,0:T(8,128)(2,1)} %param.33, f32[512,512]{1,0:T(8,128)} %param.31, f32[512,512]{1,0:T(8,128)} %param.32), kind=kLoop, calls=%fused_computation.85 | loop fusion | flops 4456448 | bytes 7340032 | tf_op jit(solution)/shard_map/convert_element_type | solution.py:99
  22.5 36.0 %all-gather.5.cloned.1.call-done = bf16[512,2,512]{2,1,0:T(2,128)(2,1)} async-done(((bf16[64,2,512]{2,1,0:T(2,128)(2,1)}), bf16[512,2,512]{2,1,0:T(2,128)(2,1)}) %all-gather.5.cloned.1.call-update) | async-done | bytes 1048592 | tf_op jit(solution)/shard_map/all_gather | solution.py:105
  58.4 5.2 %gather_fusion = bf16[512,2,512]{2,1,0:T(2,128)(2,1)} fusion(bf16[512,2,512]{2,1,0:T(2,128)(2,1)} %all-gather.5.cloned.1.call-done, s32[1024]{0:T(1024)S(1)} %pad_clamp_fusion), kind=kCustom, calls=%fused_computation | custom fusion | bytes 2099200 | tf_op jit(solution)/shard_map/jit(_take)/gather | solution.py:106
  63.6 3.6 %broadcast_select_fusion = bf16[512,2,512]{2,1,0:T(2,128)(2,1)} fusion(bf16[512,2,512]{2,1,0:T(2,128)(2,1)} %gather_fusion, pred[512]{0:T(512)(128)(4,1)S(1)} %compare_and_fusion), kind=kLoop, calls=%fused_computation.7 | loop fusion | flops 524288 | bytes 2097664 | tf_op jit(solution)/shard_map/jit(_take)/select_n | solution.py:106
  67.2 4.6 %all-to-all-start = ((bf16[512,2,512]{2,1,0:T(2,128)(2,1)}), bf16[512,2,512]{2,1,0:T(2,128)(2,1)}, u32[]{:S(2)}, u32[]{:S(2)}) async-start(bf16[512,2,512]{2,1,0:T(2,128)(2,1)} %broadcast_select_fusion), calls=%async_computation | async-start | bytes 2097152 | tf_op jit(solution)/shard_map/all_to_all | solution.py:107
  72.3 23.7 %all-to-all-done = bf16[512,2,512]{2,1,0:T(2,128)(2,1)} async-done(((bf16[512,2,512]{2,1,0:T(2,128)(2,1)}), bf16[512,2,512]{2,1,0:T(2,128)(2,1)}, u32[]{:S(2)}, u32[]{:S(2)}) %all-to-all-start) | async-done | bytes 1048608 | tf_op jit(solution)/shard_map/all_to_all | solution.py:107
  96.0 2.8 copy.72
  98.8 2.4 reshape.229
  101.2 6.0 %all-gather.9.cloned.1.call-done = bf16[8192,256]{0,1:T(8,128)(2,1)} async-done(((bf16[512,256]{0,1:T(8,128)(2,1)}), bf16[8192,256]{0,1:T(8,128)(2,1)}) %all-gather.9.cloned.1.call-update) | async-done | bytes 4194320 | tf_op jit(solution)/shard_map/all_gather | solution.py:116
  107.2 3.9 %convolution_bitcast_fusion = f32[32,2,2,1,128]{4,0,2,1,3:T(8,128)S(1)} fusion(bf16[2,128,8192,1]{2,1,0,3:T(8,128)(2,1)} %bitcast.110, bf16[32,2,8192,1]{2,0,1,3:T(8,128)(2,1)} %reshape.229), kind=kOutput, calls=%fused_computation.20 | convolution fusion | flops 268435456 | bytes 5308416 | tf_op jit(solution)/shard_map/dot_general | solution.py:114
  111.4 49.8 %all-gather.7.cloned.1.call-done = bf16[8192,512]{1,0:T(8,128)(2,1)} async-done(((bf16[512,512]{1,0:T(8,128)(2,1)}), bf16[8192,512]{1,0:T(8,128)(2,1)}) %all-gather.7.cloned.1.call-update) | async-done | bytes 8388624 | tf_op jit(solution)/shard_map/all_gather | solution.py:111
  161.3 12.0 %copy.37 = bf16[512,8192]{1,0:T(8,128)(2,1)} copy(bf16[512,8192]{0,1:T(8,128)(2,1)} %bitcast.109) | data formatting | bytes 16777216 | tf_op jit(solution)/shard_map/dot_general | solution.py:109
  173.3 6.4 %fusion.36 = f32[32,2,4,128]{3,0,2,1:T(8,128)S(1)} fusion(bf16[4,128,8192,1]{2,1,0,3:T(8,128)(2,1)} %bitcast.108, bf16[32,2,8192,1]{2,0,1,3:T(8,128)(2,1)} %reshape.229), kind=kOutput, calls=%fused_computation.29 | convolution fusion | flops 536870912 | bytes 9568256 | tf_op jit(solution)/shard_map/dot_general | solution.py:109
  179.9 0.7 fusion.73
  180.6 1.3 fusion.72
  182.7 0.8 fusion.20
  183.5 32.4 %all-gather.11.cloned.1.call-done = bf16[512,8192]{1,0:T(8,128)(2,1)} async-done(((bf16[512,512]{1,0:T(8,128)(2,1)}), bf16[512,8192]{1,0:T(8,128)(2,1)}) %all-gather.11.cloned.1.call-update) | async-done | bytes 8388624 | tf_op jit(solution)/shard_map/all_gather | solution.py:130
  215.9 6.0 %convolution_convert_fusion = bf16[32,2,8192]{2,0,1:T(8,128)(2,1)} fusion(bf16[512,8192]{1,0:T(8,128)(2,1)} %all-gather.11.cloned.1.call-done, bf16[32,2,512]{2,1,0:T(2,128)(2,1)S(1)} %convert_element_type.77), kind=kOutput, calls=%fused_computation.1 | convolution fusion | flops 537395200 | bytes 9502720 | tf_op jit(solution)/shard_map/dot_general | solution.py:128
  222.0 72.4 %reduce-scatter.2.cloned.1.call-done = bf16[32,2,1024]{2,0,1:T(8,128)(2,1)} async-done(((bf16[32,2,8192]{2,0,1:T(8,128)(2,1)}), bf16[32,2,1024]{2,0,1:T(8,128)(2,1)}) %reduce-scatter.2.cloned.1.call-update) | async-done | bytes 131088 | tf_op jit(solution)/shard_map/reduce_scatter | solution.py:134
  294.4 1.7 copy.44
  (37 shorter events, 2.1 us)
Async XLA Ops:
  7.2 173.4 %copy-start = (bf16[32,1,384,128]{3,2,1,0:T(8,128)(2,1)S(1)}, bf16[32,1,384,128]{3,2,1,0:T(8,128)(2,1)}, u32[]{:S(2)}) copy-start(bf16[32,1,384,128]{3,2,1,0:T(8,128)(2,1)} %param.19) | copy-start | bytes 9437188
  7.2 51.2 %all-gather.5.cloned.1.call-start = ((), (), s32[]{:S(2)}) async-start(), calls=%async_computation.2 | async-start | bytes 1179648 | tf_op jit(solution)/shard_map/all_gather | solution.py:105
  7.9 99.3 %all-gather.9.cloned.1.call-start = ((), (), s32[]{:S(2)}) async-start(), calls=%async_computation.4 | async-start | bytes 4456448 | tf_op jit(solution)/shard_map/all_gather | solution.py:116
  13.4 147.8 %all-gather.7.cloned.1.call-start = ((), (), s32[]{:S(2)}) async-start(), calls=%async_computation.3 | async-start | bytes 8912896 | tf_op jit(solution)/shard_map/all_gather | solution.py:111
  17.9 4.5 %copy-start.1 = (s32[512]{0:T(512)S(1)}, s32[512]{0:T(512)}, u32[]{:S(2)}) copy-start(s32[512]{0:T(512)} %param.18) | copy-start | bytes 6148
  17.9 198.0 %all-gather.11.cloned.1.call-start = ((), (), s32[]{:S(2)}) async-start(), calls=%async_computation.5 | async-start | bytes 8912896 | tf_op jit(solution)/shard_map/all_gather | solution.py:130
  22.4 49.7 %copy-start.2 = (s32[32]{0:T(128)S(1)}, s32[32]{0:T(128)}, u32[]{:S(2)}) copy-start(s32[32]{0:T(128)} %param.21) | copy-start | bytes 388
  67.2 28.8 %all-to-all-start = ((bf16[512,2,512]{2,1,0:T(2,128)(2,1)}), bf16[512,2,512]{2,1,0:T(2,128)(2,1)}, u32[]{:S(2)}, u32[]{:S(2)}) async-start(bf16[512,2,512]{2,1,0:T(2,128)(2,1)} %broadcast_select_fusion), calls=%async_computation | async-start | bytes 2097152 | tf_op jit(solution)/shard_map/all_to_all | solution.py:107
  71.8 222.6 %reduce-scatter.2.cloned.1.call-start = ((), (), s32[]{:S(2)}) async-start(), calls=%async_computation.6 | async-start | bytes 1179648 | tf_op jit(solution)/shard_map/reduce_scatter | solution.py:134
  179.6 3.0 %copy-start.3 = (bf16[32,1,384,128]{3,2,1,0:T(8,128)(2,1)S(1)}, bf16[32,1,384,128]{3,2,1,0:T(8,128)(2,1)}, u32[]{:S(2)}) copy-start(bf16[32,1,384,128]{3,2,1,0:T(8,128)(2,1)} %param.20) | copy-start | bytes 9437188
Sparse Core Ops, SparseCore 0:
  10.4 47.9 all-gather.4
  60.1 47.1 all-gather.8
  108.9 52.2 all-gather.6
  162.8 53.1 all-gather.10
  222.1 72.2 reduce-scatter.1
where the time goes:
time: 304 us; the launch traced here: 303 us
  waiting for transfers between devices  221 us (73%)
  local copies, waits for them, and re-layouts  25 us (8%)
  matrix products  19.4 us (6%)
  other arithmetic  18.2 us (6%)
  between operations  14 us (5%)
  starting transfers between devices  4.97 us (2%)
    reduce_scatter x1, waiting for transfers between devices, per_device(): lax.psum_scatter(partial_out.astype(jnp.bfloat16), 'tp', scatter_dimensio...  72.4 us
    all_gather x1, waiting for transfers between devices, per_device(): lax.all_gather(w_query, 'rep', axis=0, tiled=True)  49.8 us
    all_gather x1, waiting for transfers between devices, per_device(): gathered = lax.all_gather(tokens_x, 'tp', axis=0, tiled=True)  36 us
    all_gather x1, waiting for transfers between devices, per_device(): lax.all_gather(w_output, 'rep', axis=1, tiled=True)  32.4 us
    all_to_all x1, waiting for transfers between devices, per_device(): lax.all_to_all(ordered, 'rep', split_axis=0, concat_axis=2, tiled=True)  23.7 us
    dot_general x2, local copies, waits for them, and re-layouts, per_device(): jnp.dot(flat_rows, lax.all_gather(w_query, 'rep', axis=0, tiled=True), pr...  14.4 us
    dot_general x1, matrix products, per_device(): jnp.dot(flat_rows, lax.all_gather(w_query, 'rep', axis=0, tiled=True), pr...  6.37 us
  transfers between devices with their start and end apart: 6, of which 6 were waited for; matrix products, arithmetic and copies ran while one was open for 18% of the time, Pallas kernels for 0%

commit v1 on v0

v1 whole, which is shorter than its diff:
```python
import functools

import jax
import jax.numpy as jnp
from jax import lax
from jax.experimental import pallas as pl
from jax.experimental.pallas import tpu as pltpu
from jax.sharding import Mesh, PartitionSpec as P

learn_rate = 0.002
beta_one = 0.9
beta_two = 0.95
adam_eps = 1e-08
weight_decay = 0.1
step_count = 100.0
rope_base = 500000.0

AXES = ("z", "xl", "c", "y", "xh")
SIZES = (4, 2, 2, 4, 2)
CHIPS = ("z", "xl")
TP = ("y", "xh")
STEPS = 2
SLOTS = 32
CACHE = 384
HEAD = 128
GROUP = 4
MIB = 1024 * 1024


def adam_step(master, moment, second, gradient):
    grad_wide = gradient.astype(jnp.float32)
    new_moment = beta_one * moment + (1.0 - beta_one) * grad_wide
    new_second = beta_two * second + (1.0 - beta_two) * grad_wide * grad_wide
    moment_hat = new_moment / (1.0 - beta_one**step_count)
    second_hat = new_second / (1.0 - beta_two**step_count)
    new_master = master - learn_rate * (
        moment_hat / (jnp.sqrt(second_hat) + adam_eps) + weight_decay * master
    )
    return (new_master, new_moment, new_second)


def move(array, target):
    pairs = []
    for source in range(128):
        rest, coords = source, []
        for size in reversed(SIZES):
            rest, coord = divmod(rest, size)
            coords.append(coord)
        index = 0
        for coord, size in zip(target(*reversed(coords)), SIZES):
            index = index * size + coord % size
        pairs.append((source, index))
    return lax.ppermute(array, AXES, pairs)


def to_sibling(array):
    return move(array, lambda z, xl, c, y, xh: (z, xl, 1 - c, y, xh))


def dot(a, b):
    return jnp.dot(a, b, preferred_element_type=jnp.float32)


def params(mib):
    return pltpu.CompilerParams(vmem_limit_bytes=mib * MIB)


VMEM = pl.BlockSpec(memory_space=pltpu.VMEM)
SMEM = pl.BlockSpec(memory_space=pltpu.SMEM)
ANY = pl.BlockSpec(memory_space=pl.ANY)


def select_rows(slots, rows):
    hot = lax.broadcasted_iota(jnp.int32, (slots.shape[0], rows), 1) == slots
    return hot.astype(jnp.bfloat16)


def order_kernel(slots_ref, x_ref, out_ref):
    hot = select_rows(slots_ref[...], x_ref.shape[0])
    out_ref[...] = dot(hot, x_ref[...]).astype(jnp.bfloat16)


def own_kernel(slots_ref, x_ref, w_ref, out_ref):
    hot = select_rows(slots_ref[...], x_ref.shape[0])
    half = x_ref.shape[1] // STEPS
    for step in range(STEPS):
        ordered = dot(hot, x_ref[:, step * half : (step + 1) * half]).astype(jnp.bfloat16)
        out_ref[step] = dot(ordered, w_ref[...])


def add_kernel(own_ref, x_ref, w_ref, out_ref):
    half = x_ref.shape[1] // STEPS
    for step in range(STEPS):
        total = own_ref[step] + dot(x_ref[:, step * half : (step + 1) * half], w_ref[...])
        total = total.astype(jnp.bfloat16)
        for chip in range(8):
            out_ref[chip, step * SLOTS : (step + 1) * SLOTS, :] = total[
                chip * SLOTS : (chip + 1) * SLOTS
            ]


CHUNKS = 4
PER = SLOTS // CHUNKS
ROWS = STEPS * GROUP


def attend_kernel(
    parts_ref, cos_ref, sin_ref, len_ref, keys_ref, values_ref, out_ref,
    key_buf, value_buf, q_buf, kx_buf, vx_buf, mix_buf, att_buf, key_sem, value_sem,
):
    copies = []
    for chunk in range(CHUNKS):
        rows = pl.ds(chunk * PER, PER)
        for source, buf, sem in (
            (keys_ref, key_buf, key_sem),
            (values_ref, value_buf, value_sem),
        ):
            copy = pltpu.make_async_copy(source.at[rows], buf.at[rows], sem.at[chunk])
            copy.start()
            copies.append(copy)
    total = parts_ref[0].astype(jnp.float32)
    for chip in range(1, 8):
        total = total + parts_ref[chip].astype(jnp.float32)
    cosine = cos_ref[...]
    sine = sin_ref[...]

    def rotate(vectors):
        turned = vectors * cosine + pltpu.roll(vectors, HEAD // 2, 1) * sine
        return turned.astype(jnp.bfloat16).astype(jnp.float32)

    for head in range(GROUP):
        turned = rotate(total[:, head * HEAD : (head + 1) * HEAD])
        for step in range(STEPS):
            q_buf[pl.ds(step * GROUP + head, SLOTS, stride=ROWS), :] = turned[
                step * SLOTS : (step + 1) * SLOTS
            ]
    k_new = rotate(total[:, GROUP * HEAD : (GROUP + 1) * HEAD])
    v_new = total[:, (GROUP + 1) * HEAD :].astype(jnp.bfloat16).astype(jnp.float32)
    for step in range(STEPS):
        for row in range(ROWS):
            kx_buf[step, pl.ds(row, SLOTS, stride=ROWS), :] = k_new[
                step * SLOTS : (step + 1) * SLOTS
            ]
            vx_buf[step, pl.ds(row, SLOTS, stride=ROWS), :] = v_new[
                step * SLOTS : (step + 1) * SLOTS
            ]
    scale = 1.0 / HEAD**0.5
    many = PER * ROWS
    for chunk in range(CHUNKS):
        first = chunk * many
        q_rows = q_buf[first : first + many]
        new_zero = jnp.sum(q_rows * kx_buf[0, first : first + many], axis=-1, keepdims=True) * scale
        new_one = jnp.sum(q_rows * kx_buf[1, first : first + many], axis=-1, keepdims=True) * scale
        row = lax.broadcasted_iota(jnp.int32, (many, 1), 0)
        second_step = lax.rem(row, ROWS) >= GROUP
        new_one = jnp.where(second_step, new_one, -1e30)
        copies[2 * chunk].wait()
        scores = []
        for slot in range(PER):
            scores.append(
                lax.dot_general(
                    q_rows[slot * ROWS : (slot + 1) * ROWS].astype(jnp.bfloat16),
                    key_buf[chunk * PER + slot],
                    (((1,), (1,)), ((), ())),
                    preferred_element_type=jnp.float32,
                )
            )
        scores = jnp.concatenate(scores, axis=0) * scale
        position = lax.broadcasted_iota(jnp.int32, (many, CACHE), 1)
        scores = jnp.where(position < len_ref[first : first + many], scores, -1e30)
        top = jnp.maximum(
            jnp.max(scores, axis=-1, keepdims=True), jnp.maximum(new_zero, new_one)
        )
        scores = jnp.exp(scores - top)
        new_zero = jnp.exp(new_zero - top)
        new_one = jnp.exp(new_one - top)
        total_exp = jnp.sum(scores, axis=-1, keepdims=True) + new_zero + new_one
        scores = scores / total_exp
        new_zero = (new_zero / total_exp).astype(jnp.bfloat16).astype(jnp.float32)
        new_one = (new_one / total_exp).astype(jnp.bfloat16).astype(jnp.float32)
        copies[2 * chunk + 1].wait()
        mixed = []
        for slot in range(PER):
            mixed.append(
                dot(
                    scores[slot * ROWS : (slot + 1) * ROWS].astype(jnp.bfloat16),
                    value_buf[chunk * PER + slot],
                )
            )
        mixed = jnp.concatenate(mixed, axis=0)
        mixed = mixed + new_zero * vx_buf[0, first : first + many]
        mixed = mixed + new_one * vx_buf[1, first : first + many]
        mix_buf[first : first + many] = mixed
    for head in range(GROUP):
        for step in range(STEPS):
            att_buf[head, pl.ds(step, SLOTS, stride=STEPS), :] = mix_buf[
                pl.ds(step * GROUP + head, SLOTS, stride=ROWS), :
            ]
    for core in range(2):
        for head in range(2):
            part = att_buf[core * 2 + head].astype(jnp.bfloat16)
            for chip in range(8):
                out_ref[core * 8 + chip, :, head * HEAD : (head + 1) * HEAD] = part


def attend(parts, cosine, sine, lengths, keys, values):
    flat = SLOTS * ROWS
    return pl.pallas_call(
        attend_kernel,
        out_shape=jax.ShapeDtypeStruct((16, STEPS * SLOTS, 2 * HEAD), jnp.bfloat16),
        in_specs=[VMEM, VMEM, VMEM, VMEM, ANY, ANY],
        out_specs=VMEM,
        scratch_shapes=[
            pltpu.VMEM((SLOTS, CACHE, HEAD), jnp.bfloat16),
            pltpu.VMEM((SLOTS, CACHE, HEAD), jnp.bfloat16),
            pltpu.VMEM((flat, HEAD), jnp.float32),
            pltpu.VMEM((STEPS, flat, HEAD), jnp.float32),
            pltpu.VMEM((STEPS, flat, HEAD), jnp.float32),
            pltpu.VMEM((flat, HEAD), jnp.float32),
            pltpu.VMEM((GROUP, STEPS * SLOTS, HEAD), jnp.float32),
            pltpu.SemaphoreType.DMA((CHUNKS,)),
            pltpu.SemaphoreType.DMA((CHUNKS,)),
        ],
        compiler_params=params(32),
    )(parts, cosine, sine, lengths, keys, values)


def out_kernel(att_ref, w_ref, out_ref):
    @pl.when(pl.program_id(0) == 0)
    def _():
        out_ref[...] = jnp.zeros_like(out_ref)

    for core in range(2):
        total = out_ref[core]
        for part in range(2):
            total = total + dot(att_ref[core, part], w_ref[part])
        out_ref[core] = total


def project(att, w_all):
    return pl.pallas_call(
        out_kernel,
        grid=(4,),
        out_shape=jax.ShapeDtypeStruct((2, 64, 1024), jnp.float32),
        in_specs=[
            pl.BlockSpec((2, 2, 64, 256), lambda i: (0, i, 0, 0)),
            pl.BlockSpec((2, 256, 1024), lambda i: (i, 0, 0)),
        ],
        out_specs=pl.BlockSpec((2, 64, 1024), lambda i: (0, 0, 0)),
        compiler_params=params(16),
    )(att, w_all)


def per_device(
    tokens_x,
    slot_rows,
    cache_keys,
    cache_values,
    lengths,
    master_query,
    moment_query,
    second_query,
    gradient_query,
    master_keyval,
    moment_keyval,
    second_keyval,
    gradient_keyval,
    master_output,
    moment_output,
    second_output,
    gradient_output,
):
    core = lax.axis_index("c")

    x_own = tokens_x.reshape(64, 1024)
    x_all = lax.all_to_all(
        jnp.broadcast_to(x_own[None], (8, 64, 1024)), TP, 0, 0, tiled=True
    ).reshape(512, 1024)

    state_output = adam_step(master_output, moment_output, second_output, gradient_output)
    w_output = state_output[0].astype(jnp.bfloat16)
    halves = w_output.reshape(2, 256, 512)
    w_keep = move(
        lax.dynamic_index_in_dim(halves, core, 0, False),
        lambda z, xl, c, y, xh: (y, xh, c, z, xl),
    )
    w_cross = move(
        lax.dynamic_index_in_dim(halves, 1 - core, 0, False),
        lambda z, xl, c, y, xh: (y, xh, 1 - c, z, xl),
    )
    w_wide = jnp.where(
        core == 0,
        jnp.concatenate([w_keep, w_cross], axis=1),
        jnp.concatenate([w_cross, w_keep], axis=1),
    )
    w_all = lax.all_gather(w_wide, CHIPS, axis=0)

    state_query = adam_step(master_query, moment_query, second_query, gradient_query)
    state_keyval = adam_step(master_keyval, moment_keyval, second_keyval, gradient_keyval)
    w_own = jnp.concatenate(
        [
            state_query[0].astype(jnp.bfloat16),
            state_keyval[0].astype(jnp.bfloat16).reshape(512, 256),
        ],
        axis=1,
    )
    w_sibling = to_sibling(w_own)

    by_core = slot_rows.reshape(8, 2, SLOTS).transpose(1, 0, 2).reshape(2, 256, 1)
    mine = lax.dynamic_index_in_dim(by_core, core, 0, False)
    others = lax.dynamic_index_in_dim(by_core, 1 - core, 0, False)
    x_send = pl.pallas_call(
        order_kernel,
        out_shape=jax.ShapeDtypeStruct((256, 1024), jnp.bfloat16),
        in_specs=[VMEM] * 2,
        out_specs=VMEM,
        compiler_params=params(16),
    )(others, x_all)
    x_sibling = to_sibling(x_send)
    own = pl.pallas_call(
        own_kernel,
        out_shape=jax.ShapeDtypeStruct((STEPS, 256, 768), jnp.float32),
        in_specs=[VMEM] * 3,
        out_specs=VMEM,
        compiler_params=params(16),
    )(mine, x_all, w_own)
    parts = pl.pallas_call(
        add_kernel,
        out_shape=jax.ShapeDtypeStruct((8, STEPS * SLOTS, 768), jnp.bfloat16),
        in_specs=[VMEM] * 3,
        out_specs=VMEM,
        compiler_params=params(16),
    )(own, x_sibling, w_sibling)
    parts = lax.all_to_all(parts, CHIPS, 0, 0, tiled=True)

    positions = (
        jnp.arange(STEPS, dtype=jnp.int32)[:, None] + lengths[None, :]
    ).reshape(STEPS * SLOTS, 1)
    freqs = rope_base ** (-2.0 * jnp.arange(HEAD // 2, dtype=jnp.float32) / HEAD)
    angles = positions.astype(jnp.float32) * freqs
    cosine = jnp.cos(angles)
    sine = jnp.sin(angles)
    cosine = jnp.concatenate([cosine, cosine], axis=1)
    sine = jnp.concatenate([-sine, sine], axis=1)
    attended = attend(
        parts,
        cosine,
        sine,
        jnp.repeat(lengths, ROWS)[:, None],
        cache_keys.reshape(SLOTS, CACHE, HEAD),
        cache_values.reshape(SLOTS, CACHE, HEAD),
    )
    attended = lax.all_to_all(attended, ("c",) + TP, 0, 0, tiled=True)
    partial_out = project(attended.reshape(2, 8, 64, 256), w_all)
    arrived = to_sibling(lax.dynamic_index_in_dim(partial_out, 1 - core, 0, False))
    decoded = lax.dynamic_index_in_dim(partial_out, core, 0, False) + arrived
    decoded = decoded.astype(jnp.bfloat16).reshape(SLOTS, STEPS, 1024)
    return (
        state_query[0],
        state_query[1],
        state_query[2],
        state_keyval[0],
        state_keyval[1],
        state_keyval[2],
        state_output[0],
        state_output[1],
        state_output[2],
        decoded,
    )


def solution(mesh):
    fine = Mesh(mesh.devices.reshape(SIZES), AXES)
    rep = ("z", "xl", "c")
    tp = TP
    return jax.shard_map(
        per_device,
        mesh=fine,
        in_specs=(
            P(tp, None, rep),
            P(),
            P(rep, tp, None, None),
            P(rep, tp, None, None),
            P(rep),
            P(rep, tp),
            P(rep, tp),
            P(rep, tp),
            P(rep, tp),
            P(rep, None, tp),
            P(rep, None, tp),
            P(rep, None, tp),
            P(rep, None, tp),
            P(tp, rep),
            P(tp, rep),
            P(tp, rep),
            P(tp, rep),
        ),
        out_specs=(
            P(rep, tp),
            P(rep, tp),
            P(rep, tp),
            P(rep, None, tp),
            P(rep, None, tp),
            P(rep, None, tp),
            P(tp, rep),
            P(tp, rep),
            P(tp, rep),
            P(rep, None, tp),
        ),
        check_vma=False,
    )
```

time: 304 us -> 172 us (0.57)
  waiting for transfers between devices: 221 us -> 86.5 us
  blocking collectives: 0 us -> 20.6 us
  matrix products: 19.4 us -> 0 us
  local copies, waits for them, and re-layouts: 25 us -> 8.7 us
  starting transfers between devices: 4.97 us -> 19.9 us
  Pallas kernels: 0 us -> 10.1 us
  other arithmetic: 18.2 us -> 10.8 us
    all_gather x4 -> x1, waiting for transfers between devices: 124 us -> 20.8 us  [per_device(): w_all = lax.all_gather(w_wide, CHIPS, axis=0)]
    reduce_scatter x1 -> x0, waiting for transfers between devices: 72.4 us -> none  [per_device(): lax.psum_scatter(partial_out.astype(jnp.bfloat16), 'tp', scatter_dimensio...]
    ppermute x0 -> x5, waiting for transfers between devices: none -> 24.4 us  [move(): return lax.ppermute(array, AXES, pairs)]
    all_to_all x0 -> x1, blocking collectives: none -> 20.6 us  [per_device(): attended = lax.all_to_all(attended, ('c',) + TP, 0, 0, tiled=True)]
    dot_general x7 -> x0, matrix products: 19.4 us -> none  [the longest x1 6.37 us: per_device(): jnp.dot(flat_rows, lax.all_gather(w_query, 'rep', axis=0, tiled=True), pr...]
    all_to_all x1 -> x2, waiting for transfers between devices: 23.7 us -> 41.2 us  [the longest x1 21.8 us: per_device(): parts = lax.all_to_all(parts, CHIPS, 0, 0, tiled=True)]
    dot_general x2 -> x0, local copies, waits for them, and re-layouts: 14.4 us -> none  [per_device(): jnp.dot(flat_rows, lax.all_gather(w_query, 'rep', axis=0, tiled=True), pr...]
    pallas_call x0 -> x5, Pallas kernels: none -> 10.1 us  [the longest x1 4.11 us: attend(): pl.pallas_call(attend_kernel, out_shape=jax.ShapeDtypeStruct((16, STEPS *...]
  transfers between devices with their start and end apart: 6 -> 8, of which waited for: 6 -> 7; matrix products, arithmetic and copies ran while one was open for 18% -> 4% of each run, Pallas kernels for 0% -> 5%
where the time goes in v1:
time: 172 us; the launch traced here: 171 us
  waiting for transfers between devices  86.5 us (50%)
  blocking collectives  20.6 us (12%)
  starting transfers between devices  19.9 us (12%)
  between operations  14.3 us (8%)
  other arithmetic  10.8 us (6%)
  Pallas kernels  10.1 us (6%)
  local copies, waits for them, and re-layouts  8.7 us (5%)
    ppermute x5, waiting for transfers between devices, move(): return lax.ppermute(array, AXES, pairs)  24.4 us
    all_to_all x1, waiting for transfers between devices, per_device(): parts = lax.all_to_all(parts, CHIPS, 0, 0, tiled=True)  21.8 us
    all_gather x1, waiting for transfers between devices, per_device(): w_all = lax.all_gather(w_wide, CHIPS, axis=0)  20.8 us
    all_to_all x1, blocking collectives, per_device(): attended = lax.all_to_all(attended, ('c',) + TP, 0, 0, tiled=True)  20.6 us
    all_to_all x1, waiting for transfers between devices, per_device(): lax.all_to_all(jnp.broadcast_to(x_own[None], (8, 64, 1024)), TP, 0, 0, ti...  19.4 us
    ppermute x5, starting transfers between devices, move(): return lax.ppermute(array, AXES, pairs)  8.9 us
    all_to_all x1, starting transfers between devices, per_device(): lax.all_to_all(jnp.broadcast_to(x_own[None], (8, 64, 1024)), TP, 0, 0, ti...  6.9 us
    unnamed x30, local copies, waits for them, and re-layouts  6.09 us
  transfers between devices with their start and end apart: 8, of which 7 were waited for; matrix products, arithmetic and copies ran while one was open for 4% of the time, Pallas kernels for 5%

profile of v1, /device:TPU:24, one launch (start us, length us, event | category | flops | bytes accessed | tf_op | source)
XLA Modules:
  0.0 170.8 jit_solution(12963275212831626806)
XLA Ops:
  7.2 4.2 %fusion.10 = (bf16[512,512]{1,0:T(8,128)(2,1)S(1)}, f32[512,512]{1,0:T(8,128)}, f32[512,512]{1,0:T(8,128)}, f32[512,512]{1,0:T(8,128)}) fusion(f32[512,512]{1,0:T(8,128)} %param.30, bf16[512,512]{1,0:T(8,128)(2,1)} %param.33, f32[512,512]{1,0:T(8,128)} %param.31, f32[512,512]{1,0:T(8,128)} %param.32), kind=kLoop, calls=%fused_computation.34 | loop fusion | flops 4456448 | bytes 7340032 | tf_op jit(solution)/shard_map/convert_element_type | solution.py:281
  11.5 5.7 %collective-permute-start.2 = (bf16[256,512]{1,0:T(8,128)(2,1)S(1)}, bf16[256,512]{1,0:T(8,128)(2,1)S(1)}, u32[]{:S(2)}, u32[]{:S(2)}) collective-permute-start(bf16[256,512]{1,0:T(8,128)(2,1)S(1)} %get-tuple-element.22), channel_id=1, source_target_pairs={{0,0},{1,16},{2,32},{3,48},{4,64},{5,80},{6,96},{7,112},{8,8},{9,2... | collective-permute-start | bytes 786440 | tf_op jit(solution)/shard_map/ppermute | solution.py:53
  18.1 18.1 %collective-permute-done.2 = bf16[256,512]{1,0:T(8,128)(2,1)S(1)} collective-permute-done((bf16[256,512]{1,0:T(8,128)(2,1)S(1)}, bf16[256,512]{1,0:T(8,128)(2,1)S(1)}, u32[]{:S(2)}, u32[]{:S(2)}) %collective-permute-start.2) | collective-permute-done | bytes 262176 | tf_op jit(solution)/shard_map/ppermute | solution.py:53
  36.2 4.4 %collective-permute-done.3 = bf16[256,512]{1,0:T(8,128)(2,1)S(1)} collective-permute-done((bf16[256,512]{1,0:T(8,128)(2,1)S(1)}, bf16[256,512]{1,0:T(8,128)(2,1)S(1)}, u32[]{:S(2)}, u32[]{:S(2)}) %collective-permute-start.3) | collective-permute-done | bytes 262176 | tf_op jit(solution)/shard_map/ppermute | solution.py:53
  40.6 0.9 maximum_select_fusion
  41.7 1.1 broadcast_in_dim.14
  42.8 6.9 %all-to-all-start = ((bf16[8,64,1024]{2,1,0:T(8,128)(2,1)}), bf16[8,64,1024]{2,1,0:T(8,128)(2,1)S(1)}, u32[]{:S(2)}, u32[]{:S(2)}) async-start(bf16[8,64,1024]{2,1,0:T(8,128)(2,1)} %broadcast_in_dim.14), calls=%async_computation | async-start | bytes 2097152 | tf_op jit(solution)/shard_map/all_to_all | solution.py:276
  49.8 3.0 %fusion.16 = (bf16[512,2,128]{2,1,0:T(2,128)(2,1)S(1)}, f32[512,2,128]{2,1,0:T(2,128)}, f32[512,2,128]{2,1,0:T(2,128)}, f32[512,2,128]{2,1,0:T(2,128)}) fusion(f32[512,2,128]{2,1,0:T(2,128)S(1)} %copy-done.7, bf16[512,2,128]{2,1,0:T(2,128)(2,1)S(1)} %copy-done.10, f32[512,2,128]{2,1,0:T(2,128)S(1)} %copy-done.8, f32[512,2,128]{2,1,0:T(2,128)S(1)} %copy-done.9), kind=kLoop, calls=%fused_computation.36 | loop fusion | flops 2228224 | bytes 3670016 | tf_op jit(solution)/shard_map/convert_element_type | solution.py:303
  52.8 2.2 %fusion.13 = (bf16[512,512]{1,0:T(8,128)(2,1)S(1)}, f32[512,512]{1,0:T(8,128)}, f32[512,512]{1,0:T(8,128)}, f32[512,512]{1,0:T(8,128)}) fusion(f32[512,512]{1,0:T(8,128)S(1)} %copy-done.3, bf16[512,512]{1,0:T(8,128)(2,1)S(1)} %copy-done.6, f32[512,512]{1,0:T(8,128)S(1)} %copy-done.4, f32[512,512]{1,0:T(8,128)S(1)} %copy-done.5), kind=kLoop, calls=%fused_computation.35 | loop fusion | flops 4456448 | bytes 7340032 | tf_op jit(solution)/shard_map/convert_element_type | solution.py:302
  55.1 1.5 collective-permute-start.1
  56.9 19.4 %all-to-all-done = bf16[8,64,1024]{2,1,0:T(8,128)(2,1)S(1)} async-done(((bf16[8,64,1024]{2,1,0:T(8,128)(2,1)}), bf16[8,64,1024]{2,1,0:T(8,128)(2,1)S(1)}, u32[]{:S(2)}, u32[]{:S(2)}) %all-to-all-start) | async-done | bytes 1048608 | tf_op jit(solution)/shard_map/all_to_all | solution.py:276
  76.3 1.3 shard_map.241
  78.5 1.1 shard_map.240.own_ref
  80.1 1.5 shard_map.242
  81.5 4.0 %all-to-all-start.1 = ((bf16[8,64,768]{2,1,0:T(8,128)(2,1)}), bf16[8,64,768]{2,1,0:T(8,128)(2,1)S(1)}, u32[]{:S(2)}, u32[]{:S(2)}) async-start(bf16[8,64,768]{2,1,0:T(8,128)(2,1)} %shard_map.242), calls=%async_computation.1 | async-start | bytes 1572864 | tf_op jit(solution)/shard_map/all_to_all | solution.py:334
  86.2 21.8 %all-to-all-done.1.parts_ref = bf16[8,64,768]{2,1,0:T(8,128)(2,1)S(1)} async-done(((bf16[8,64,768]{2,1,0:T(8,128)(2,1)}), bf16[8,64,768]{2,1,0:T(8,128)(2,1)S(1)}, u32[]{:S(2)}, u32[]{:S(2)}) %all-to-all-start.1) | async-done | bytes 786464 | tf_op jit(solution)/shard_map/all_to_all | solution.py:334
  107.9 1.9 %copy-done.1 = bf16[32,1,384,128]{3,2,1,0:T(8,128)(2,1)S(1)} copy-done((bf16[32,1,384,128]{3,2,1,0:T(8,128)(2,1)S(1)}, bf16[32,1,384,128]{3,2,1,0:T(8,128)(2,1)}, u32[]{:S(2)}) %copy-start.1) | copy-done | bytes 3145752
  109.8 1.9 %copy-done.2 = bf16[32,1,384,128]{3,2,1,0:T(8,128)(2,1)S(1)} copy-done((bf16[32,1,384,128]{3,2,1,0:T(8,128)(2,1)S(1)}, bf16[32,1,384,128]{3,2,1,0:T(8,128)(2,1)}, u32[]{:S(2)}) %copy-start.2) | copy-done | bytes 3145752
  111.7 4.1 %shard_map.243 = bf16[16,64,256]{2,1,0:T(8,128)(2,1)S(1)} custom-call(bf16[8,64,768]{2,1,0:T(8,128)(2,1)S(1)} %all-to-all-done.1.parts_ref, f32[64,128]{1,0:T(8,128)S(1)} %get-tuple-element.29.cos_ref, f32[64,128]{1,0:T(8,128)S(1)} %get-tuple-element.30.sin_ref, s32[256,1]{1,0:T(8,128)S(1)} %broadcast_in_dim_reshape.5.len_ref, ...), custom_call_target="tpu_custom_call" | custom-call | tf_op jit(solution)/shard_map/pallas_call | solution.py:208
  115.9 20.6 %all_to_all.15 = bf16[16,64,256]{2,1,0:T(8,128)(2,1)S(1)} all-to-all(bf16[16,64,256]{2,1,0:T(8,128)(2,1)S(1)} %shard_map.243), channel_id=1, replica_groups=mesh['z'=4,'xl'=2,'c'=2,'y'=4,'xh'=2] {'c','y','xh'}, dimensions={0} | all-to-all | bytes 1048576 | tf_op jit(solution)/shard_map/all_to_all | solution.py:353
  136.5 20.8 %all-gather.2.cloned.1.call-done.w_ref = bf16[8,256,1024]{2,1,0:T(8,128)(2,1)} async-done(((bf16[1,256,1024]{2,1,0:T(8,128)(2,1)}), bf16[8,256,1024]{2,1,0:T(8,128)(2,1)}) %all-gather.2.cloned.1.call-update) | async-done | bytes 4194320 | tf_op jit(solution)/shard_map/all_gather | solution.py:296
  157.3 2.2 %copy-done = bf16[8,256,1024]{2,1,0:T(8,128)(2,1)S(1)} copy-done((bf16[8,256,1024]{2,1,0:T(8,128)(2,1)S(1)}, bf16[8,256,1024]{2,1,0:T(8,128)(2,1)}, u32[]{:S(2)}) %copy-start) | copy-done | bytes 4194328
  159.5 2.1 %shard_map.244 = f32[2,64,1024]{2,1,0:T(8,128)S(1)} custom-call(bf16[2,8,64,256]{3,2,1,0:T(8,128)(2,1)S(1)} %bitcast.32, bf16[8,256,1024]{2,1,0:T(8,128)(2,1)S(1)} %copy-done), custom_call_target="tpu_custom_call" | custom-call | tf_op jit(solution)/shard_map/pallas_call | solution.py:241
  161.7 1.5 collective-permute-done.4
  (52 shorter events, 4.2 us)
Async XLA Ops:
  7.2 150.1 %all-gather.2.cloned.1.call-start = ((), (), s32[]{:S(2)}) async-start(), calls=%async_computation.3 | async-start | bytes 4718592 | tf_op jit(solution)/shard_map/all_gather | solution.py:296
  11.5 30.1 %copy-start.11 = (bf16[64,2,512]{2,1,0:T(2,128)(2,1)S(1)}, bf16[64,2,512]{2,1,0:T(2,128)(2,1)}, u32[]{:S(2)}) copy-start(bf16[64,2,512]{2,1,0:T(2,128)(2,1)} %param.17) | copy-start | bytes 393220
  11.5 24.7 %collective-permute-start.2 = (bf16[256,512]{1,0:T(8,128)(2,1)S(1)}, bf16[256,512]{1,0:T(8,128)(2,1)S(1)}, u32[]{:S(2)}, u32[]{:S(2)}) collective-permute-start(bf16[256,512]{1,0:T(8,128)(2,1)S(1)} %get-tuple-element.22), channel_id=1, source_target_pairs={{0,0},{1,16},{2,32},{3,48},{4,64},{5,80},{6,96},{7,112},{8,8},{9,2... | collective-permute-start | bytes 786440 | tf_op jit(solution)/shard_map/ppermute | solution.py:53
  17.2 23.3 %collective-permute-start.3 = (bf16[256,512]{1,0:T(8,128)(2,1)S(1)}, bf16[256,512]{1,0:T(8,128)(2,1)S(1)}, u32[]{:S(2)}, u32[]{:S(2)}) collective-permute-start(bf16[256,512]{1,0:T(8,128)(2,1)S(1)} %get-tuple-element.23), channel_id=1, source_target_pairs={{0,8},{1,24},{2,40},{3,56},{4,72},{5,88},{6,104},{7,120},{8,0},{9,... | collective-permute-start | bytes 786440 | tf_op jit(solution)/shard_map/ppermute | solution.py:53
  41.6 8.1 %copy-start.7 = (f32[512,2,128]{2,1,0:T(2,128)S(1)}, f32[512,2,128]{2,1,0:T(2,128)}, u32[]{:S(2)}) copy-start(f32[512,2,128]{2,1,0:T(2,128)} %param.26) | copy-start | bytes 1572868
  41.6 8.1 %copy-start.8 = (f32[512,2,128]{2,1,0:T(2,128)S(1)}, f32[512,2,128]{2,1,0:T(2,128)}, u32[]{:S(2)}) copy-start(f32[512,2,128]{2,1,0:T(2,128)} %param.27) | copy-start | bytes 1572868
  41.6 8.1 %copy-start.9 = (f32[512,2,128]{2,1,0:T(2,128)S(1)}, f32[512,2,128]{2,1,0:T(2,128)}, u32[]{:S(2)}) copy-start(f32[512,2,128]{2,1,0:T(2,128)} %param.28) | copy-start | bytes 1572868
  41.6 8.1 %copy-start.10 = (bf16[512,2,128]{2,1,0:T(2,128)(2,1)S(1)}, bf16[512,2,128]{2,1,0:T(2,128)(2,1)}, u32[]{:S(2)}) copy-start(bf16[512,2,128]{2,1,0:T(2,128)(2,1)} %param.29) | copy-start | bytes 786436
  42.8 33.5 %all-to-all-start = ((bf16[8,64,1024]{2,1,0:T(8,128)(2,1)}), bf16[8,64,1024]{2,1,0:T(8,128)(2,1)S(1)}, u32[]{:S(2)}, u32[]{:S(2)}) async-start(bf16[8,64,1024]{2,1,0:T(8,128)(2,1)} %broadcast_in_dim.14), calls=%async_computation | async-start | bytes 2097152 | tf_op jit(solution)/shard_map/all_to_all | solution.py:276
  49.7 3.0 %copy-start.3 = (f32[512,512]{1,0:T(8,128)S(1)}, f32[512,512]{1,0:T(8,128)}, u32[]{:S(2)}) copy-start(f32[512,512]{1,0:T(8,128)} %param.22) | copy-start | bytes 3145732
  49.7 3.0 %copy-start.4 = (f32[512,512]{1,0:T(8,128)S(1)}, f32[512,512]{1,0:T(8,128)}, u32[]{:S(2)}) copy-start(f32[512,512]{1,0:T(8,128)} %param.23) | copy-start | bytes 3145732
  49.7 3.0 %copy-start.5 = (f32[512,512]{1,0:T(8,128)S(1)}, f32[512,512]{1,0:T(8,128)}, u32[]{:S(2)}) copy-start(f32[512,512]{1,0:T(8,128)} %param.24) | copy-start | bytes 3145732
  49.8 3.0 %copy-start.6 = (bf16[512,512]{1,0:T(8,128)(2,1)S(1)}, bf16[512,512]{1,0:T(8,128)(2,1)}, u32[]{:S(2)}) copy-start(bf16[512,512]{1,0:T(8,128)(2,1)} %param.25) | copy-start | bytes 1572868
  55.0 1.5 copy-start.12
  55.1 24.4 %collective-permute-start.1 = (bf16[512,768]{1,0:T(8,128)(2,1)S(1)}, bf16[512,768]{1,0:T(8,128)(2,1)S(1)}, u32[]{:S(2)}, u32[]{:S(2)}) collective-permute-start(bf16[512,768]{1,0:T(8,128)(2,1)S(1)} %pad_maximum_fusion.w_ref), channel_id=1, source_target_pairs={{0,8},{1,9},{2,10},{3,11},{4,12},{5,13},{6,14},{7,15},{8,0},{9,1},... | collective-permute-start | bytes 2359304 | tf_op jit(solution)/shard_map/ppermute | solution.py:53
  77.6 2.4 %collective-permute-start = (bf16[256,1024]{1,0:T(8,128)(2,1)}, bf16[256,1024]{1,0:T(8,128)(2,1)S(1)}, u32[]{:S(2)}, u32[]{:S(2)}) collective-permute-start(bf16[256,1024]{1,0:T(8,128)(2,1)} %shard_map.241), channel_id=1, source_target_pairs={{0,8},{1,9},{2,10},{3,11},{4,12},{5,13},{6,14},{7,15},{8,0},{9,1},... | collective-permute-start | bytes 1572872 | tf_op jit(solution)/shard_map/ppermute | solution.py:53
  81.5 4.1 %copy-start.13 = (s32[32]{0:T(128)S(1)}, s32[32]{0:T(128)}, u32[]{:S(2)}) copy-start(s32[32]{0:T(128)} %param.21) | copy-start | bytes 388
  81.5 26.4 %all-to-all-start.1 = ((bf16[8,64,768]{2,1,0:T(8,128)(2,1)}), bf16[8,64,768]{2,1,0:T(8,128)(2,1)S(1)}, u32[]{:S(2)}, u32[]{:S(2)}) async-start(bf16[8,64,768]{2,1,0:T(8,128)(2,1)} %shard_map.242), calls=%async_computation.1 | async-start | bytes 1572864 | tf_op jit(solution)/shard_map/all_to_all | solution.py:334
  107.9 1.9 %copy-start.1 = (bf16[32,1,384,128]{3,2,1,0:T(8,128)(2,1)S(1)}, bf16[32,1,384,128]{3,2,1,0:T(8,128)(2,1)}, u32[]{:S(2)}) copy-start(bf16[32,1,384,128]{3,2,1,0:T(8,128)(2,1)} %param.19) | copy-start | bytes 9437188
  109.8 1.9 %copy-start.2 = (bf16[32,1,384,128]{3,2,1,0:T(8,128)(2,1)S(1)}, bf16[32,1,384,128]{3,2,1,0:T(8,128)(2,1)}, u32[]{:S(2)}) copy-start(bf16[32,1,384,128]{3,2,1,0:T(8,128)(2,1)} %param.20) | copy-start | bytes 9437188
  157.3 2.2 %copy-start = (bf16[8,256,1024]{2,1,0:T(8,128)(2,1)S(1)}, bf16[8,256,1024]{2,1,0:T(8,128)(2,1)}, u32[]{:S(2)}) copy-start(bf16[8,256,1024]{2,1,0:T(8,128)(2,1)} %all-gather.2.cloned.1.call-done.w_ref) | copy-start | bytes 12582916
  161.6 1.6 collective-permute-start.4
Sparse Core Ops, SparseCore 0:
  41.7 115.5 all-gather.1

commit v2 on v1

--- a/solution.py
+++ b/solution.py
@@ -24,6 +24,7 @@
 CACHE = 384
 HEAD = 128
 GROUP = 4
+OUTPUT = 512
 MIB = 1024 * 1024
 
 
@@ -57,6 +58,10 @@
     return move(array, lambda z, xl, c, y, xh: (z, xl, 1 - c, y, xh))
 
 
+def transpose(array):
+    return move(array, lambda z, xl, c, y, xh: (y, xh, c, z, xl))
+
+
 def dot(a, b):
     return jnp.dot(a, b, preferred_element_type=jnp.float32)
 
@@ -67,7 +72,7 @@
 
 VMEM = pl.BlockSpec(memory_space=pltpu.VMEM)
 SMEM = pl.BlockSpec(memory_space=pltpu.SMEM)
-ANY = pl.BlockSpec(memory_space=pl.ANY)
+HBM = pl.BlockSpec(memory_space=pltpu.HBM)
 
 
 def select_rows(slots, rows):
@@ -85,13 +90,14 @@
     half = x_ref.shape[1] // STEPS
     for step in range(STEPS):
         ordered = dot(hot, x_ref[:, step * half : (step + 1) * half]).astype(jnp.bfloat16)
-        out_ref[step] = dot(ordered, w_ref[...])
-
-
-def add_kernel(own_ref, x_ref, w_ref, out_ref):
+        out_ref[step] = dot(ordered, w_ref[:, OUTPUT:])
+
+
+def add_kernel(own_ref, x_ref, w_ref, cos_ref, sin_ref, len_ref, out_ref):
+    del cos_ref, sin_ref, len_ref
     half = x_ref.shape[1] // STEPS
     for step in range(STEPS):
-        total = own_ref[step] + dot(x_ref[:, step * half : (step + 1) * half], w_ref[...])
+        total = own_ref[step] + dot(x_ref[:, step * half : (step + 1) * half], w_ref[:, OUTPUT:])
         total = total.astype(jnp.bfloat16)
         for chip in range(8):
             out_ref[chip, step * SLOTS : (step + 1) * SLOTS, :] = total[
@@ -99,9 +105,10 @@
             ]
 
 
-CHUNKS = 4
+CHUNKS = 2
 PER = SLOTS // CHUNKS
 ROWS = STEPS * GROUP
+AHEAD = 2
 
 
 def attend_kernel(
@@ -111,13 +118,15 @@
     copies = []
     for chunk in range(CHUNKS):
         rows = pl.ds(chunk * PER, PER)
-        for source, buf, sem in (
-            (keys_ref, key_buf, key_sem),
-            (values_ref, value_buf, value_sem),
-        ):
-            copy = pltpu.make_async_copy(source.at[rows], buf.at[rows], sem.at[chunk])
-            copy.start()
-            copies.append(copy)
+        copies.append(
+            (
+                pltpu.make_async_copy(keys_ref.at[rows], key_buf.at[rows], key_sem.at[chunk]),
+                pltpu.make_async_copy(values_ref.at[rows], value_buf.at[rows], value_sem.at[chunk]),
+            )
+        )
+    for chunk in range(AHEAD):
+        copies[chunk][0].start()
+        copies[chunk][1].start()
     total = parts_ref[0].astype(jnp.float32)
     for chip in range(1, 8):
         total = total + parts_ref[chip].astype(jnp.float32)
@@ -154,7 +163,10 @@
         row = lax.broadcasted_iota(jnp.int32, (many, 1), 0)
         second_step = lax.rem(row, ROWS) >= GROUP
         new_one = jnp.where(second_step, new_one, -1e30)
-        copies[2 * chunk].wait()
+        copies[chunk][0].wait()
+        if chunk + AHEAD < CHUNKS:
+            copies[chunk + AHEAD][0].start()
+            copies[chunk + AHEAD][1].start()
         scores = []
         for slot in range(PER):
             scores.append(
@@ -178,7 +190,7 @@
         scores = scores / total_exp
         new_zero = (new_zero / total_exp).astype(jnp.bfloat16).astype(jnp.float32)
         new_one = (new_one / total_exp).astype(jnp.bfloat16).astype(jnp.float32)
-        copies[2 * chunk + 1].wait()
+        copies[chunk][1].wait()
         mixed = []
         for slot in range(PER):
             mixed.append(
@@ -196,19 +208,22 @@
             att_buf[head, pl.ds(step, SLOTS, stride=STEPS), :] = mix_buf[
                 pl.ds(step * GROUP + head, SLOTS, stride=ROWS), :
             ]
-    for core in range(2):
-        for head in range(2):
-            part = att_buf[core * 2 + head].astype(jnp.bfloat16)
-            for chip in range(8):
-                out_ref[core * 8 + chip, :, head * HEAD : (head + 1) * HEAD] = part
+    for head in range(GROUP):
+        part = att_buf[head].astype(jnp.bfloat16)
+        for chip in range(8):
+            out_ref[chip, :, head * HEAD : (head + 1) * HEAD] = part
+
+
+def in_hbm(array):
+    return pltpu.with_memory_space_constraint(array, pltpu.HBM)
 
 
 def attend(parts, cosine, sine, lengths, keys, values):
     flat = SLOTS * ROWS
     return pl.pallas_call(
         attend_kernel,
-        out_shape=jax.ShapeDtypeStruct((16, STEPS * SLOTS, 2 * HEAD), jnp.bfloat16),
-        in_specs=[VMEM, VMEM, VMEM, VMEM, ANY, ANY],
+        out_shape=jax.ShapeDtypeStruct((8, STEPS * SLOTS, GROUP * HEAD), jnp.bfloat16),
+        in_specs=[VMEM, VMEM, VMEM, VMEM, HBM, HBM],
         out_specs=VMEM,
         scratch_shapes=[
             pltpu.VMEM((SLOTS, CACHE, HEAD), jnp.bfloat16),
@@ -221,34 +236,33 @@
             pltpu.SemaphoreType.DMA((CHUNKS,)),
             pltpu.SemaphoreType.DMA((CHUNKS,)),
         ],
-        compiler_params=params(32),
+        compiler_params=params(16),
     )(parts, cosine, sine, lengths, keys, values)
 
 
-def out_kernel(att_ref, w_ref, out_ref):
-    @pl.when(pl.program_id(0) == 0)
-    def _():
-        out_ref[...] = jnp.zeros_like(out_ref)
-
-    for core in range(2):
-        total = out_ref[core]
-        for part in range(2):
-            total = total + dot(att_ref[core, part], w_ref[part])
-        out_ref[core] = total
-
-
-def project(att, w_all):
+def out_kernel(core_ref, att_ref, own_ref, sibling_ref, out_ref):
+    core = core_ref[0]
+    for w_ref, half in ((own_ref, core), (sibling_ref, 1 - core)):
+        product = dot(att_ref[...], w_ref[...]).astype(jnp.bfloat16)
+        columns = pl.ds(pl.multiple_of(half * 512, 512), 512)
+        for chip in range(8):
+            out_ref[chip, :, columns] = product[chip * 64 : (chip + 1) * 64]
+
+
+def project(core, att, own, sibling):
     return pl.pallas_call(
         out_kernel,
-        grid=(4,),
-        out_shape=jax.ShapeDtypeStruct((2, 64, 1024), jnp.float32),
+        out_shape=jax.ShapeDtypeStruct((8, 64, 1024), jnp.bfloat16),
+        grid=(1,),
         in_specs=[
-            pl.BlockSpec((2, 2, 64, 256), lambda i: (0, i, 0, 0)),
-            pl.BlockSpec((2, 256, 1024), lambda i: (i, 0, 0)),
+            SMEM,
+            pl.BlockSpec((512, 512), lambda i: (0, 0)),
+            pl.BlockSpec((512, OUTPUT), lambda i: (0, 0)),
+            pl.BlockSpec((512, OUTPUT), lambda i: (0, 0)),
         ],
-        out_specs=pl.BlockSpec((2, 64, 1024), lambda i: (0, 0, 0)),
+        out_specs=pl.BlockSpec((8, 64, 1024), lambda i: (0, 0, 0)),
         compiler_params=params(16),
-    )(att, w_all)
+    )(core, att, own, sibling)
 
 
 def per_device(
@@ -279,26 +293,11 @@
 
     state_output = adam_step(master_output, moment_output, second_output, gradient_output)
     w_output = state_output[0].astype(jnp.bfloat16)
-    halves = w_output.reshape(2, 256, 512)
-    w_keep = move(
-        lax.dynamic_index_in_dim(halves, core, 0, False),
-        lambda z, xl, c, y, xh: (y, xh, c, z, xl),
-    )
-    w_cross = move(
-        lax.dynamic_index_in_dim(halves, 1 - core, 0, False),
-        lambda z, xl, c, y, xh: (y, xh, 1 - c, z, xl),
-    )
-    w_wide = jnp.where(
-        core == 0,
-        jnp.concatenate([w_keep, w_cross], axis=1),
-        jnp.concatenate([w_cross, w_keep], axis=1),
-    )
-    w_all = lax.all_gather(w_wide, CHIPS, axis=0)
-
     state_query = adam_step(master_query, moment_query, second_query, gradient_query)
     state_keyval = adam_step(master_keyval, moment_keyval, second_keyval, gradient_keyval)
     w_own = jnp.concatenate(
         [
+            w_output,
             state_query[0].astype(jnp.bfloat16),
             state_keyval[0].astype(jnp.bfloat16).reshape(512, 256),
         ],
@@ -324,15 +323,6 @@
         out_specs=VMEM,
         compiler_params=params(16),
     )(mine, x_all, w_own)
-    parts = pl.pallas_call(
-        add_kernel,
-        out_shape=jax.ShapeDtypeStruct((8, STEPS * SLOTS, 768), jnp.bfloat16),
-        in_specs=[VMEM] * 3,
-        out_specs=VMEM,
-        compiler_params=params(16),
-    )(own, x_sibling, w_sibling)
-    parts = lax.all_to_all(parts, CHIPS, 0, 0, tiled=True)
-
     positions = (
         jnp.arange(STEPS, dtype=jnp.int32)[:, None] + lengths[None, :]
     ).reshape(STEPS * SLOTS, 1)
@@ -342,19 +332,29 @@
     sine = jnp.sin(angles)
     cosine = jnp.concatenate([cosine, cosine], axis=1)
     sine = jnp.concatenate([-sine, sine], axis=1)
+    length_rows = jnp.repeat(lengths, ROWS)[:, None]
+    parts = pl.pallas_call(
+        add_kernel,
+        out_shape=jax.ShapeDtypeStruct((8, STEPS * SLOTS, 768), jnp.bfloat16),
+        in_specs=[VMEM] * 6,
+        out_specs=VMEM,
+        compiler_params=params(16),
+    )(own, x_sibling, w_sibling, cosine, sine, length_rows)
+    parts = lax.all_to_all(parts, CHIPS, 0, 0, tiled=True)
+
     attended = attend(
         parts,
         cosine,
         sine,
-        jnp.repeat(lengths, ROWS)[:, None],
-        cache_keys.reshape(SLOTS, CACHE, HEAD),
-        cache_values.reshape(SLOTS, CACHE, HEAD),
+        length_rows,
+        in_hbm(cache_keys.reshape(SLOTS, CACHE, HEAD)),
+        in_hbm(cache_values.reshape(SLOTS, CACHE, HEAD)),
     )
-    attended = lax.all_to_all(attended, ("c",) + TP, 0, 0, tiled=True)
-    partial_out = project(attended.reshape(2, 8, 64, 256), w_all)
-    arrived = to_sibling(lax.dynamic_index_in_dim(partial_out, 1 - core, 0, False))
-    decoded = lax.dynamic_index_in_dim(partial_out, core, 0, False) + arrived
-    decoded = decoded.astype(jnp.bfloat16).reshape(SLOTS, STEPS, 1024)
+    attended = lax.all_to_all(attended, CHIPS, 0, 0, tiled=True).reshape(512, 512)
+    partial_out = project(core.reshape(1), attended, w_own, w_sibling)
+    partial_out = lax.all_to_all(partial_out, TP, 0, 0, tiled=True)
+    decoded = jnp.sum(partial_out.astype(jnp.float32), axis=0).astype(jnp.bfloat16)
+    decoded = transpose(decoded).reshape(SLOTS, STEPS, 1024)
     return (
         state_query[0],
         state_query[1],

time: 172 us -> 98.3 us (0.57)
  waiting for transfers between devices: 86.5 us -> 11.3 us
  blocking collectives: 20.6 us -> 49.4 us
  between operations: 14.3 us -> 0.86 us
  starting transfers between devices: 19.9 us -> 11.8 us
  local copies, waits for them, and re-layouts: 8.7 us -> 3.64 us
    all_to_all x1 -> x3, blocking collectives: 20.6 us -> 49.4 us  [the longest x1 18.7 us: per_device(): partial_out = lax.all_to_all(partial_out, TP, 0, 0, tiled=True)]
    all_to_all x1 -> x0, waiting for transfers between devices: 21.8 us -> none  [per_device(): parts = lax.all_to_all(parts, CHIPS, 0, 0, tiled=True)]
    all_gather x1 -> x0, waiting for transfers between devices: 20.8 us -> none  [per_device(): w_all = lax.all_gather(w_wide, CHIPS, axis=0)]
    ppermute x5 -> x3, waiting for transfers between devices: 24.4 us -> 6.57 us  [move(): return lax.ppermute(array, AXES, pairs)]
    all_to_all x1, waiting for transfers between devices: 19.4 us -> 4.73 us  [per_device(): lax.all_to_all(jnp.broadcast_to(x_own[None], (8, 64, 1024)), TP, 0, 0, ti...]
    unnamed x30 -> x18, local copies, waits for them, and re-layouts: 6.09 us -> 1.15 us
    ppermute x5 -> x3, starting transfers between devices: 8.9 us -> 4.67 us  [move(): return lax.ppermute(array, AXES, pairs)]
    all_to_all x1 -> x0, starting transfers between devices: 4.05 us -> none  [per_device(): parts = lax.all_to_all(parts, CHIPS, 0, 0, tiled=True)]
  transfers between devices with their start and end apart: 8 -> 4, of which waited for: 7 -> 3; matrix products, arithmetic and copies ran while one was open for 4% -> 11% of each run, Pallas kernels for 5% -> 2%
where the time goes in v2:
time: 98.3 us; the launch traced here: 98 us
  blocking collectives  49.4 us (50%)
  starting transfers between devices  11.8 us (12%)
  waiting for transfers between devices  11.3 us (11%)
  Pallas kernels  11 us (11%)
  other arithmetic  9.99 us (10%)
  local copies, waits for them, and re-layouts  3.64 us (4%)
    all_to_all x1, blocking collectives, per_device(): partial_out = lax.all_to_all(partial_out, TP, 0, 0, tiled=True)  18.7 us
    all_to_all x1, blocking collectives, per_device(): parts = lax.all_to_all(parts, CHIPS, 0, 0, tiled=True)  18.4 us
    all_to_all x1, blocking collectives, per_device(): lax.all_to_all(attended, CHIPS, 0, 0, tiled=True).reshape(512, 512)  12.2 us
    all_to_all x1, starting transfers between devices, per_device(): lax.all_to_all(jnp.broadcast_to(x_own[None], (8, 64, 1024)), TP, 0, 0, ti...  7.15 us
    ppermute x3, waiting for transfers between devices, move(): return lax.ppermute(array, AXES, pairs)  6.57 us
    convert_element_type x1, other arithmetic, per_device(): w_output = state_output[0].astype(jnp.bfloat16)  6.47 us
    pallas_call x1, Pallas kernels, attend(): pl.pallas_call(attend_kernel, out_shape=jax.ShapeDtypeStruct((8, STEPS *...  4.95 us
    all_to_all x1, waiting for transfers between devices, per_device(): lax.all_to_all(jnp.broadcast_to(x_own[None], (8, 64, 1024)), TP, 0, 0, ti...  4.73 us
  transfers between devices with their start and end apart: 4, of which 3 were waited for; matrix products, arithmetic and copies ran while one was open for 11% of the time, Pallas kernels for 2%

profile of v2, /device:TPU:24, one launch (start us, length us, event | category | flops | bytes accessed | tf_op | source)
XLA Modules:
  0.0 98.0 jit_solution(12225011341589739292)
XLA Ops:
  0.7 1.1 %copy.34 = bf16[8,8,2,512]{3,1,2,0:T(8,128)(2,1)S(1)} copy(bf16[8,8,2,512]{3,2,1,0:T(2,128)(2,1)} %bitcast.24) | data formatting | bytes 262144
  1.7 1.1 %broadcast_in_dim.14 = bf16[8,64,1024]{2,1,0:T(8,128)(2,1)} broadcast(bf16[64,1024]{1,0:T(8,128)(2,1)S(1)} %bitcast.23), dimensions={1,2} | broadcast | bytes 1179648 | tf_op jit(solution)/shard_map/broadcast_in_dim | solution.py:291
  2.8 7.2 %all-to-all-start = ((bf16[8,64,1024]{2,1,0:T(8,128)(2,1)}), bf16[8,64,1024]{2,1,0:T(8,128)(2,1)S(1)}, u32[]{:S(2)}, u32[]{:S(2)}) async-start(bf16[8,64,1024]{2,1,0:T(8,128)(2,1)} %broadcast_in_dim.14), calls=%async_computation | async-start | bytes 2097152 | tf_op jit(solution)/shard_map/all_to_all | solution.py:290
  10.0 6.5 %fusion.7 = (bf16[512,512]{1,0:T(8,128)(2,1)S(1)}, f32[512,512]{1,0:T(8,128)}, f32[512,512]{1,0:T(8,128)}, f32[512,512]{1,0:T(8,128)}, bf16[512,512]{1,0:T(8,128...) fusion(f32[512,512]{1,0:T(8,128)S(1)} %copy-done, bf16[512,512]{1,0:T(8,128)(2,1)} %param.33, ...), kind=kLoop, calls=%fused_computation.26 | loop fusion | flops 8912896 | bytes 14680064 | tf_op jit(solution)/shard_map/convert_element_type | solution.py:295
  16.5 3.0 %fusion.13 = (bf16[512,2,128]{2,1,0:T(2,128)(2,1)S(1)}, f32[512,2,128]{2,1,0:T(2,128)}, f32[512,2,128]{2,1,0:T(2,128)}, f32[512,2,128]{2,1,0:T(2,128)}) fusion(f32[512,2,128]{2,1,0:T(2,128)S(1)} %copy-done.2, bf16[512,2,128]{2,1,0:T(2,128)(2,1)S(1)} %copy-done.5, f32[512,2,128]{2,1,0:T(2,128)S(1)} %copy-done.3, f32[512,2,128]{2,1,0:T(2,128)S(1)} %copy-done.4), kind=kLoop, calls=%fused_computation.28 | loop fusion | flops 2228224 | bytes 3670016 | tf_op jit(solution)/shard_map/convert_element_type | solution.py:302
  19.5 0.1 pad_maximum_fusion.w_ref.own_ref
  19.9 0.1 copy.31.slots_ref
  20.1 4.7 %all-to-all-done = bf16[8,64,1024]{2,1,0:T(8,128)(2,1)S(1)} async-done(((bf16[8,64,1024]{2,1,0:T(8,128)(2,1)}), bf16[8,64,1024]{2,1,0:T(8,128)(2,1)S(1)}, u32[]{:S(2)}, u32[]{:S(2)}) %all-to-all-start) | async-done | bytes 1048608 | tf_op jit(solution)/shard_map/all_to_all | solution.py:290
  24.8 1.3 %shard_map.241 = bf16[256,1024]{1,0:T(8,128)(2,1)} custom-call(s32[256,1]{1,0:T(8,128)S(1)} %copy.31.slots_ref, bf16[512,1024]{1,0:T(8,128)(2,1)S(1)} %bitcast.16), custom_call_target="tpu_custom_call" | custom-call | tf_op jit(solution)/shard_map/pallas_call | solution.py:311
  26.3 0.1 broadcast_in_dim_reshape.5.len_ref
  26.4 0.1 copy.30.slots_ref
  26.5 0.2 fusion.6
  26.8 1.1 %shard_map.240.own_ref = f32[2,256,768]{2,1,0:T(8,128)S(1)} custom-call(s32[256,1]{1,0:T(8,128)S(1)} %copy.30.slots_ref, bf16[512,1024]{1,0:T(8,128)(2,1)S(1)} %bitcast.17, bf16[512,1280]{1,0:T(8,128)(2,1)S(1)} %pad_maximum_fusion.w_ref.own_ref), custom_call_target="tpu_custom_call" | custom-call | tf_op jit(solution)/shard_map/pallas_call | solution.py:319
  27.9 0.3 collective-permute-done.x_ref
  28.2 1.9 %shard_map.242 = bf16[8,64,768]{2,1,0:T(8,128)(2,1)S(1)} custom-call(f32[2,256,768]{2,1,0:T(8,128)S(1)} %shard_map.240.own_ref, bf16[256,1024]{1,0:T(8,128)(2,1)S(1)} %collective-permute-done.x_ref, bf16[512,1280]{1,0:T(8,128)(2,1)} %collective-permute-done.1.w_ref.sibling_ref, f32[64,128]{1,0:T(8,128)S(1)} %get-tuple-element.31.cos_ref, ...), custom_call_target="tpu_custom_call" | custom-call | tf_op jit(solution)/shard_map/pallas_call | solution.py:336
  30.1 18.4 %all_to_all.20.parts_ref = bf16[8,64,768]{2,1,0:T(8,128)(2,1)S(1)} all-to-all(bf16[8,64,768]{2,1,0:T(8,128)(2,1)S(1)} %shard_map.242), channel_id=1, replica_groups=mesh['z'=4,'xl'=2,'c'=2,'y'=4,'xh'=2] {'z','xl'}, dimensions={0} | all-to-all | bytes 1572864 | tf_op jit(solution)/shard_map/all_to_all | solution.py:343
  48.5 4.9 %shard_map.243 = bf16[8,64,512]{2,1,0:T(8,128)(2,1)S(1)} custom-call(bf16[8,64,768]{2,1,0:T(8,128)(2,1)S(1)} %all_to_all.20.parts_ref, f32[64,128]{1,0:T(8,128)S(1)} %get-tuple-element.31.cos_ref, f32[64,128]{1,0:T(8,128)S(1)} %get-tuple-element.32.sin_ref, s32[256,1]{1,0:T(8,128)S(1)} %broadcast_in_dim_reshape.5.len_ref, bf16[32,384,128]{2,1,0:T(8,128)(2,1)} %bitcast.19, ...), custom_call_target="tpu_custom_call" | custom-call | tf_op jit(solution)/shard_map/pallas_call | solution.py:223
  53.5 12.2 %all_to_all.21 = bf16[8,64,512]{2,1,0:T(8,128)(2,1)S(1)} all-to-all(bf16[8,64,512]{2,1,0:T(8,128)(2,1)S(1)} %shard_map.243), channel_id=1, replica_groups=mesh['z'=4,'xl'=2,'c'=2,'y'=4,'xh'=2] {'z','xl'}, dimensions={0} | all-to-all | bytes 1048576 | tf_op jit(solution)/shard_map/all_to_all | solution.py:353
  65.7 1.8 %shard_map.244 = bf16[8,64,1024]{2,1,0:T(8,128)(2,1)S(1)} custom-call(s32[1]{0:T(128)} %bitcast.core_ref, bf16[512,512]{1,0:T(8,128)(2,1)S(1)} %bitcast.18, bf16[512,1280]{1,0:T(8,128)(2,1)S(1)} %pad_maximum_fusion.w_ref.own_ref, bf16[512,1280]{1,0:T(8,128)(2,1)} %collective-permute-done.1.w_ref.sibling_ref), custom_call_target="tpu_custom_call" | custom-call | tf_op jit(solution)/shard_map/pallas_call | solution.py:253
  67.5 18.7 %all_to_all.22 = bf16[8,64,1024]{2,1,0:T(8,128)(2,1)S(1)} all-to-all(bf16[8,64,1024]{2,1,0:T(8,128)(2,1)S(1)} %shard_map.244), channel_id=1, replica_groups=mesh['z'=4,'xl'=2,'c'=2,'y'=4,'xh'=2] {'y','xh'}, dimensions={0} | all-to-all | bytes 2097152 | tf_op jit(solution)/shard_map/all_to_all | solution.py:355
  86.2 0.2 reduce_sum.12
  86.4 4.6 %collective-permute-start.2 = (bf16[64,1024]{1,0:T(8,128)(2,1)S(1)}, bf16[64,1024]{1,0:T(8,128)(2,1)S(1)}, u32[]{:S(2)}, u32[]{:S(2)}) collective-permute-start(bf16[64,1024]{1,0:T(8,128)(2,1)S(1)} %reduce_sum.12), channel_id=1, source_target_pairs={{0,0},{1,16},{2,32},{3,48},{4,64},{5,80},{6,96},{7,112},{8,8},{9,2... | collective-permute-start | bytes 393224 | tf_op jit(solution)/shard_map/ppermute | solution.py:54
  91.0 6.3 %collective-permute-done.2 = bf16[64,1024]{1,0:T(8,128)(2,1)S(1)} collective-permute-done((bf16[64,1024]{1,0:T(8,128)(2,1)S(1)}, bf16[64,1024]{1,0:T(8,128)(2,1)S(1)}, u32[]{:S(2)}, u32[]{:S(2)}) %collective-permute-start.2) | collective-permute-done | bytes 131104 | tf_op jit(solution)/shard_map/ppermute | solution.py:54
  97.2 0.7 reshape.79
  (29 shorter events, 0.6 us)
Async XLA Ops:
  0.6 9.3 %copy-start.1 = (f32[512,512]{1,0:T(8,128)S(1)}, f32[512,512]{1,0:T(8,128)}, u32[]{:S(2)}) copy-start(f32[512,512]{1,0:T(8,128)} %param.31) | copy-start | bytes 3145732
  0.7 9.3 %copy-start = (f32[512,512]{1,0:T(8,128)S(1)}, f32[512,512]{1,0:T(8,128)}, u32[]{:S(2)}) copy-start(f32[512,512]{1,0:T(8,128)} %param.30) | copy-start | bytes 3145732
  2.8 22.0 %all-to-all-start = ((bf16[8,64,1024]{2,1,0:T(8,128)(2,1)}), bf16[8,64,1024]{2,1,0:T(8,128)(2,1)S(1)}, u32[]{:S(2)}, u32[]{:S(2)}) async-start(bf16[8,64,1024]{2,1,0:T(8,128)(2,1)} %broadcast_in_dim.14), calls=%async_computation | async-start | bytes 2097152 | tf_op jit(solution)/shard_map/all_to_all | solution.py:290
  10.0 6.5 %copy-start.2 = (f32[512,2,128]{2,1,0:T(2,128)S(1)}, f32[512,2,128]{2,1,0:T(2,128)}, u32[]{:S(2)}) copy-start(f32[512,2,128]{2,1,0:T(2,128)} %param.26) | copy-start | bytes 1572868
  10.0 6.5 %copy-start.3 = (f32[512,2,128]{2,1,0:T(2,128)S(1)}, f32[512,2,128]{2,1,0:T(2,128)}, u32[]{:S(2)}) copy-start(f32[512,2,128]{2,1,0:T(2,128)} %param.27) | copy-start | bytes 1572868
  10.0 6.5 %copy-start.4 = (f32[512,2,128]{2,1,0:T(2,128)S(1)}, f32[512,2,128]{2,1,0:T(2,128)}, u32[]{:S(2)}) copy-start(f32[512,2,128]{2,1,0:T(2,128)} %param.28) | copy-start | bytes 1572868
  10.0 6.5 %copy-start.5 = (bf16[512,2,128]{2,1,0:T(2,128)(2,1)S(1)}, bf16[512,2,128]{2,1,0:T(2,128)(2,1)}, u32[]{:S(2)}) copy-start(bf16[512,2,128]{2,1,0:T(2,128)(2,1)} %param.29) | copy-start | bytes 786436
  16.5 3.2 %copy-start.6 = (s32[512]{0:T(512)S(1)}, s32[512]{0:T(512)}, u32[]{:S(2)}) copy-start(s32[512]{0:T(512)} %param.18) | copy-start | bytes 6148
  19.5 6.6 %copy-start.7 = (s32[32]{0:T(128)S(1)}, s32[32]{0:T(128)}, u32[]{:S(2)}) copy-start(s32[32]{0:T(128)} %param.21) | copy-start | bytes 388
  19.6 8.3 %collective-permute-start.1 = (bf16[512,1280]{1,0:T(8,128)(2,1)S(1)}, bf16[512,1280]{1,0:T(8,128)(2,1)}, u32[]{:S(2)}, u32[]{:S(2)}) collective-permute-start(bf16[512,1280]{1,0:T(8,128)(2,1)S(1)} %pad_maximum_fusion.w_ref.own_ref), channel_id=1, source_target_pairs={{0,8},{1,9},{2,10},{3,11},{4,12},{5,13},{6,14},{7,15},{8,0},{9,1},... | collective-permute-start | bytes 3932168 | tf_op jit(solution)/shard_map/ppermute | solution.py:54
  26.1 2.1 %collective-permute-start = (bf16[256,1024]{1,0:T(8,128)(2,1)}, bf16[256,1024]{1,0:T(8,128)(2,1)S(1)}, u32[]{:S(2)}, u32[]{:S(2)}) collective-permute-start(bf16[256,1024]{1,0:T(8,128)(2,1)} %shard_map.241), channel_id=1, source_target_pairs={{0,8},{1,9},{2,10},{3,11},{4,12},{5,13},{6,14},{7,15},{8,0},{9,1},... | collective-permute-start | bytes 1572872 | tf_op jit(solution)/shard_map/ppermute | solution.py:54
  86.4 10.9 %collective-permute-start.2 = (bf16[64,1024]{1,0:T(8,128)(2,1)S(1)}, bf16[64,1024]{1,0:T(8,128)(2,1)S(1)}, u32[]{:S(2)}, u32[]{:S(2)}) collective-permute-start(bf16[64,1024]{1,0:T(8,128)(2,1)S(1)} %reduce_sum.12), channel_id=1, source_target_pairs={{0,0},{1,16},{2,32},{3,48},{4,64},{5,80},{6,96},{7,112},{8,8},{9,2... | collective-permute-start | bytes 393224 | tf_op jit(solution)/shard_map/ppermute | solution.py:54

commit v3 on v2

--- a/solution.py
+++ b/solution.py
@@ -24,7 +24,6 @@
 CACHE = 384
 HEAD = 128
 GROUP = 4
-OUTPUT = 512
 MIB = 1024 * 1024
 
 
@@ -72,7 +71,7 @@
 
 VMEM = pl.BlockSpec(memory_space=pltpu.VMEM)
 SMEM = pl.BlockSpec(memory_space=pltpu.SMEM)
-HBM = pl.BlockSpec(memory_space=pltpu.HBM)
+ANY = pl.BlockSpec(memory_space=pl.ANY)
 
 
 def select_rows(slots, rows):
@@ -90,14 +89,14 @@
     half = x_ref.shape[1] // STEPS
     for step in range(STEPS):
         ordered = dot(hot, x_ref[:, step * half : (step + 1) * half]).astype(jnp.bfloat16)
-        out_ref[step] = dot(ordered, w_ref[:, OUTPUT:])
-
-
-def add_kernel(own_ref, x_ref, w_ref, cos_ref, sin_ref, len_ref, out_ref):
-    del cos_ref, sin_ref, len_ref
+        out_ref[step] = dot(ordered, w_ref[...])
+
+
+def add_kernel(own_ref, x_ref, w_ref, cos_ref, sin_ref, len_ref, after_ref, out_ref):
+    del cos_ref, sin_ref, len_ref, after_ref
     half = x_ref.shape[1] // STEPS
     for step in range(STEPS):
-        total = own_ref[step] + dot(x_ref[:, step * half : (step + 1) * half], w_ref[:, OUTPUT:])
+        total = own_ref[step] + dot(x_ref[:, step * half : (step + 1) * half], w_ref[...])
         total = total.astype(jnp.bfloat16)
         for chip in range(8):
             out_ref[chip, step * SLOTS : (step + 1) * SLOTS, :] = total[
@@ -108,25 +107,12 @@
 CHUNKS = 2
 PER = SLOTS // CHUNKS
 ROWS = STEPS * GROUP
-AHEAD = 2
 
 
 def attend_kernel(
-    parts_ref, cos_ref, sin_ref, len_ref, keys_ref, values_ref, out_ref,
-    key_buf, value_buf, q_buf, kx_buf, vx_buf, mix_buf, att_buf, key_sem, value_sem,
+    parts_ref, cos_ref, sin_ref, len_ref, key_buf, value_buf, out_ref,
+    q_buf, kx_buf, vx_buf, mix_buf, att_buf,
 ):
-    copies = []
-    for chunk in range(CHUNKS):
-        rows = pl.ds(chunk * PER, PER)
-        copies.append(
-            (
-                pltpu.make_async_copy(keys_ref.at[rows], key_buf.at[rows], key_sem.at[chunk]),
-                pltpu.make_async_copy(values_ref.at[rows], value_buf.at[rows], value_sem.at[chunk]),
-            )
-        )
-    for chunk in range(AHEAD):
-        copies[chunk][0].start()
-        copies[chunk][1].start()
     total = parts_ref[0].astype(jnp.float32)
     for chip in range(1, 8):
         total = total + parts_ref[chip].astype(jnp.float32)
@@ -163,10 +149,6 @@
         row = lax.broadcasted_iota(jnp.int32, (many, 1), 0)
         second_step = lax.rem(row, ROWS) >= GROUP
         new_one = jnp.where(second_step, new_one, -1e30)
-        copies[chunk][0].wait()
-        if chunk + AHEAD < CHUNKS:
-            copies[chunk + AHEAD][0].start()
-            copies[chunk + AHEAD][1].start()
         scores = []
         for slot in range(PER):
             scores.append(
@@ -190,7 +172,6 @@
         scores = scores / total_exp
         new_zero = (new_zero / total_exp).astype(jnp.bfloat16).astype(jnp.float32)
         new_one = (new_one / total_exp).astype(jnp.bfloat16).astype(jnp.float32)
-        copies[chunk][1].wait()
         mixed = []
         for slot in range(PER):
             mixed.append(
@@ -214,29 +195,21 @@
             out_ref[chip, :, head * HEAD : (head + 1) * HEAD] = part
 
 
-def in_hbm(array):
-    return pltpu.with_memory_space_constraint(array, pltpu.HBM)
-
-
 def attend(parts, cosine, sine, lengths, keys, values):
     flat = SLOTS * ROWS
     return pl.pallas_call(
         attend_kernel,
         out_shape=jax.ShapeDtypeStruct((8, STEPS * SLOTS, GROUP * HEAD), jnp.bfloat16),
-        in_specs=[VMEM, VMEM, VMEM, VMEM, HBM, HBM],
+        in_specs=[VMEM] * 6,
         out_specs=VMEM,
         scratch_shapes=[
-            pltpu.VMEM((SLOTS, CACHE, HEAD), jnp.bfloat16),
-            pltpu.VMEM((SLOTS, CACHE, HEAD), jnp.bfloat16),
             pltpu.VMEM((flat, HEAD), jnp.float32),
             pltpu.VMEM((STEPS, flat, HEAD), jnp.float32),
             pltpu.VMEM((STEPS, flat, HEAD), jnp.float32),
             pltpu.VMEM((flat, HEAD), jnp.float32),
             pltpu.VMEM((GROUP, STEPS * SLOTS, HEAD), jnp.float32),
-            pltpu.SemaphoreType.DMA((CHUNKS,)),
-            pltpu.SemaphoreType.DMA((CHUNKS,)),
         ],
-        compiler_params=params(16),
+        compiler_params=params(12),
     )(parts, cosine, sine, lengths, keys, values)
 
 
@@ -253,14 +226,8 @@
     return pl.pallas_call(
         out_kernel,
         out_shape=jax.ShapeDtypeStruct((8, 64, 1024), jnp.bfloat16),
-        grid=(1,),
-        in_specs=[
-            SMEM,
-            pl.BlockSpec((512, 512), lambda i: (0, 0)),
-            pl.BlockSpec((512, OUTPUT), lambda i: (0, 0)),
-            pl.BlockSpec((512, OUTPUT), lambda i: (0, 0)),
-        ],
-        out_specs=pl.BlockSpec((8, 64, 1024), lambda i: (0, 0, 0)),
+        in_specs=[SMEM, VMEM, VMEM, VMEM],
+        out_specs=VMEM,
         compiler_params=params(16),
     )(core, att, own, sibling)
 
@@ -297,13 +264,14 @@
     state_keyval = adam_step(master_keyval, moment_keyval, second_keyval, gradient_keyval)
     w_own = jnp.concatenate(
         [
-            w_output,
             state_query[0].astype(jnp.bfloat16),
             state_keyval[0].astype(jnp.bfloat16).reshape(512, 256),
         ],
         axis=1,
     )
+    w_own, w_output = lax.optimization_barrier((w_own, w_output))
     w_sibling = to_sibling(w_own)
+    w_output_sibling = to_sibling(w_output)
 
     by_core = slot_rows.reshape(8, 2, SLOTS).transpose(1, 0, 2).reshape(2, 256, 1)
     mine = lax.dynamic_index_in_dim(by_core, core, 0, False)
@@ -336,10 +304,10 @@
     parts = pl.pallas_call(
         add_kernel,
         out_shape=jax.ShapeDtypeStruct((8, STEPS * SLOTS, 768), jnp.bfloat16),
-        in_specs=[VMEM] * 6,
+        in_specs=[VMEM] * 6 + [ANY],
         out_specs=VMEM,
         compiler_params=params(16),
-    )(own, x_sibling, w_sibling, cosine, sine, length_rows)
+    )(own, x_sibling, w_sibling, cosine, sine, length_rows, w_output_sibling)
     parts = lax.all_to_all(parts, CHIPS, 0, 0, tiled=True)
 
     attended = attend(
@@ -347,11 +315,11 @@
         cosine,
         sine,
         length_rows,
-        in_hbm(cache_keys.reshape(SLOTS, CACHE, HEAD)),
-        in_hbm(cache_values.reshape(SLOTS, CACHE, HEAD)),
+        cache_keys.reshape(SLOTS, CACHE, HEAD),
+        cache_values.reshape(SLOTS, CACHE, HEAD),
     )
     attended = lax.all_to_all(attended, CHIPS, 0, 0, tiled=True).reshape(512, 512)
-    partial_out = project(core.reshape(1), attended, w_own, w_sibling)
+    partial_out = project(core.reshape(1), attended, w_output, w_output_sibling)
     partial_out = lax.all_to_all(partial_out, TP, 0, 0, tiled=True)
     decoded = jnp.sum(partial_out.astype(jnp.float32), axis=0).astype(jnp.bfloat16)
     decoded = transpose(decoded).reshape(SLOTS, STEPS, 1024)

time: 98.3 us -> 94.2 us (0.958)
  Pallas kernels: 11 us -> 7.01 us
    pallas_call x1, Pallas kernels: 4.95 us -> 1.93 us  [attend(): pl.pallas_call(attend_kernel, out_shape=jax.ShapeDtypeStruct((8, STEPS *...]
    convert_element_type x1, other arithmetic: 2.95 us -> 4.25 us  [per_device(): state_keyval[0].astype(jnp.bfloat16).reshape(512, 256)]
    pallas_call x1, Pallas kernels: 1.77 us -> 0.71 us  [project(): pl.pallas_call(out_kernel, out_shape=jax.ShapeDtypeStruct((8, 64, 1024),...]
    convert_element_type x1, other arithmetic: 6.47 us -> 5.41 us  [per_device(): w_output = state_output[0].astype(jnp.bfloat16)]
    ppermute x3 -> x4, starting transfers between devices: 4.67 us -> 5.17 us  [move(): return lax.ppermute(array, AXES, pairs)]
    ppermute x3 -> x4, waiting for transfers between devices: 6.57 us -> 6.69 us  [move(): return lax.ppermute(array, AXES, pairs)]
  transfers between devices with their start and end apart: 4 -> 5, of which waited for: 3 -> 3; matrix products, arithmetic and copies ran while one was open for 11% -> 11% of each run, Pallas kernels for 2% -> 3%
where the time goes in v3:
time: 94.2 us; the launch traced here: 93.9 us
  blocking collectives  49.1 us (52%)
  starting transfers between devices  12.4 us (13%)
  waiting for transfers between devices  10.7 us (11%)
  other arithmetic  10.2 us (11%)
  Pallas kernels  7.01 us (7%)
  local copies, waits for them, and re-layouts  3.56 us (4%)
    all_to_all x1, blocking collectives, per_device(): partial_out = lax.all_to_all(partial_out, TP, 0, 0, tiled=True)  18.6 us
    all_to_all x1, blocking collectives, per_device(): parts = lax.all_to_all(parts, CHIPS, 0, 0, tiled=True)  18.3 us
    all_to_all x1, blocking collectives, per_device(): lax.all_to_all(attended, CHIPS, 0, 0, tiled=True).reshape(512, 512)  12.1 us
    all_to_all x1, starting transfers between devices, per_device(): lax.all_to_all(jnp.broadcast_to(x_own[None], (8, 64, 1024)), TP, 0, 0, ti...  7.28 us
    ppermute x4, waiting for transfers between devices, move(): return lax.ppermute(array, AXES, pairs)  6.69 us
    convert_element_type x1, other arithmetic, per_device(): w_output = state_output[0].astype(jnp.bfloat16)  5.41 us
    ppermute x4, starting transfers between devices, move(): return lax.ppermute(array, AXES, pairs)  5.17 us
    convert_element_type x1, other arithmetic, per_device(): state_keyval[0].astype(jnp.bfloat16).reshape(512, 256)  4.25 us
  transfers between devices with their start and end apart: 5, of which 3 were waited for; matrix products, arithmetic and copies ran while one was open for 11% of the time, Pallas kernels for 3%

profile of v3, /device:TPU:24, one launch (start us, length us, event | category | flops | bytes accessed | tf_op | source)
XLA Modules:
  0.0 93.9 jit_solution(17500861760807707357)
XLA Ops:
  0.6 0.9 copy.34
  1.6 1.1 %broadcast_in_dim.14 = bf16[8,64,1024]{2,1,0:T(8,128)(2,1)} broadcast(bf16[64,1024]{1,0:T(8,128)(2,1)S(1)} %bitcast.23), dimensions={1,2} | broadcast | bytes 1179648 | tf_op jit(solution)/shard_map/broadcast_in_dim | solution.py:258
  2.7 7.3 %all-to-all-start = ((bf16[8,64,1024]{2,1,0:T(8,128)(2,1)}), bf16[8,64,1024]{2,1,0:T(8,128)(2,1)S(1)}, u32[]{:S(2)}, u32[]{:S(2)}) async-start(bf16[8,64,1024]{2,1,0:T(8,128)(2,1)} %broadcast_in_dim.14), calls=%async_computation | async-start | bytes 2097152 | tf_op jit(solution)/shard_map/all_to_all | solution.py:257
  10.0 4.2 %fusion.13 = (bf16[512,2,128]{2,1,0:T(2,128)(2,1)S(1)}, f32[512,2,128]{2,1,0:T(2,128)}, f32[512,2,128]{2,1,0:T(2,128)}, f32[512,2,128]{2,1,0:T(2,128)}) fusion(f32[512,2,128]{2,1,0:T(2,128)S(1)} %copy-done.7, bf16[512,2,128]{2,1,0:T(2,128)(2,1)S(1)} %copy-done.8, f32[512,2,128]{2,1,0:T(2,128)} %param.27, f32[512,2,128]{2,1,0:T(2,128)} %param.28), kind=kLoop, calls=%fused_computation.28 | loop fusion | flops 2228224 | bytes 3670016 | tf_op jit(solution)/shard_map/convert_element_type | solution.py:268
  14.4 5.4 %fusion.7 = (bf16[512,512]{1,0:T(8,128)(2,1)S(1)}, f32[512,512]{1,0:T(8,128)}, f32[512,512]{1,0:T(8,128)}, f32[512,512]{1,0:T(8,128)}, bf16[512,512]{1,0:T(8,128...) fusion(f32[512,512]{1,0:T(8,128)S(1)} %copy-done.2, bf16[512,512]{1,0:T(8,128)(2,1)} %param.33, ...), kind=kLoop, calls=%fused_computation.26 | loop fusion | flops 8912896 | bytes 14680064 | tf_op jit(solution)/shard_map/convert_element_type | solution.py:262
  19.9 0.5 collective-permute-start.2
  20.6 0.1 copy.31.slots_ref
  20.8 4.0 %all-to-all-done = bf16[8,64,1024]{2,1,0:T(8,128)(2,1)S(1)} async-done(((bf16[8,64,1024]{2,1,0:T(8,128)(2,1)}), bf16[8,64,1024]{2,1,0:T(8,128)(2,1)S(1)}, u32[]{:S(2)}, u32[]{:S(2)}) %all-to-all-start) | async-done | bytes 1048608 | tf_op jit(solution)/shard_map/all_to_all | solution.py:257
  24.8 1.3 %shard_map.241 = bf16[256,1024]{1,0:T(8,128)(2,1)} custom-call(s32[256,1]{1,0:T(8,128)S(1)} %copy.31.slots_ref, bf16[512,1024]{1,0:T(8,128)(2,1)S(1)} %bitcast.16), custom_call_target="tpu_custom_call" | custom-call | tf_op jit(solution)/shard_map/pallas_call | solution.py:279
  26.1 0.1 copy.30.slots_ref
  26.4 0.1 broadcast_in_dim_reshape.5.len_ref
  26.5 0.2 fusion.6
  26.8 1.1 %shard_map.240.own_ref = f32[2,256,768]{2,1,0:T(8,128)S(1)} custom-call(s32[256,1]{1,0:T(8,128)S(1)} %copy.30.slots_ref, bf16[512,1024]{1,0:T(8,128)(2,1)S(1)} %bitcast.17, bf16[512,768]{1,0:T(8,128)(2,1)S(1)} %pad_maximum_fusion.w_ref), custom_call_target="tpu_custom_call" | custom-call | tf_op jit(solution)/shard_map/pallas_call | solution.py:287
  27.9 0.4 collective-permute-done.x_ref
  28.3 2.0 %shard_map.242 = bf16[8,64,768]{2,1,0:T(8,128)(2,1)S(1)} custom-call(f32[2,256,768]{2,1,0:T(8,128)S(1)} %shard_map.240.own_ref, bf16[256,1024]{1,0:T(8,128)(2,1)} %collective-permute-done.x_ref, bf16[512,768]{1,0:T(8,128)(2,1)} %collective-permute-done.1.w_ref, f32[64,128]{1,0:T(8,128)S(1)} %get-tuple-element.31.cos_ref, ...), custom_call_target="tpu_custom_call" | custom-call | tf_op jit(solution)/shard_map/pallas_call | solution.py:304
  30.4 18.3 %all_to_all.20.parts_ref = bf16[8,64,768]{2,1,0:T(8,128)(2,1)S(1)} all-to-all(bf16[8,64,768]{2,1,0:T(8,128)(2,1)S(1)} %shard_map.242), channel_id=1, replica_groups=mesh['z'=4,'xl'=2,'c'=2,'y'=4,'xh'=2] {'z','xl'}, dimensions={0} | all-to-all | bytes 1572864 | tf_op jit(solution)/shard_map/all_to_all | solution.py:311
  48.7 1.9 %shard_map.243 = bf16[8,64,512]{2,1,0:T(8,128)(2,1)S(1)} custom-call(bf16[8,64,768]{2,1,0:T(8,128)(2,1)S(1)} %all_to_all.20.parts_ref, f32[64,128]{1,0:T(8,128)S(1)} %get-tuple-element.31.cos_ref, f32[64,128]{1,0:T(8,128)S(1)} %get-tuple-element.32.sin_ref, s32[256,1]{1,0:T(8,128)S(1)} %broadcast_in_dim_reshape.5.len_ref, ...), custom_call_target="tpu_custom_call" | custom-call | tf_op jit(solution)/shard_map/pallas_call | solution.py:200
  50.6 12.1 %all_to_all.21 = bf16[8,64,512]{2,1,0:T(8,128)(2,1)S(1)} all-to-all(bf16[8,64,512]{2,1,0:T(8,128)(2,1)S(1)} %shard_map.243), channel_id=1, replica_groups=mesh['z'=4,'xl'=2,'c'=2,'y'=4,'xh'=2] {'z','xl'}, dimensions={0} | all-to-all | bytes 1048576 | tf_op jit(solution)/shard_map/all_to_all | solution.py:321
  62.8 0.7 shard_map.244
  63.5 18.6 %all_to_all.22 = bf16[8,64,1024]{2,1,0:T(8,128)(2,1)S(1)} all-to-all(bf16[8,64,1024]{2,1,0:T(8,128)(2,1)S(1)} %shard_map.244), channel_id=1, replica_groups=mesh['z'=4,'xl'=2,'c'=2,'y'=4,'xh'=2] {'y','xh'}, dimensions={0} | all-to-all | bytes 2097152 | tf_op jit(solution)/shard_map/all_to_all | solution.py:323
  82.1 0.2 reduce_sum.12
  82.3 4.6 %collective-permute-start.3 = (bf16[64,1024]{1,0:T(8,128)(2,1)S(1)}, bf16[64,1024]{1,0:T(8,128)(2,1)S(1)}, u32[]{:S(2)}, u32[]{:S(2)}) collective-permute-start(bf16[64,1024]{1,0:T(8,128)(2,1)S(1)} %reduce_sum.12), channel_id=1, source_target_pairs={{0,0},{1,16},{2,32},{3,48},{4,64},{5,80},{6,96},{7,112},{8,8},{9,2... | collective-permute-start | bytes 393224 | tf_op jit(solution)/shard_map/ppermute | solution.py:53
  86.9 6.3 %collective-permute-done.3 = bf16[64,1024]{1,0:T(8,128)(2,1)S(1)} collective-permute-done((bf16[64,1024]{1,0:T(8,128)(2,1)S(1)}, bf16[64,1024]{1,0:T(8,128)(2,1)S(1)}, u32[]{:S(2)}, u32[]{:S(2)}) %collective-permute-start.3) | collective-permute-done | bytes 131104 | tf_op jit(solution)/shard_map/ppermute | solution.py:53
  93.2 0.7 reshape.79
  (37 shorter events, 0.7 us)
Async XLA Ops:
  1.6 8.4 %copy-start.7 = (f32[512,2,128]{2,1,0:T(2,128)S(1)}, f32[512,2,128]{2,1,0:T(2,128)}, u32[]{:S(2)}) copy-start(f32[512,2,128]{2,1,0:T(2,128)} %param.26) | copy-start | bytes 1572868
  1.6 8.4 %copy-start.8 = (bf16[512,2,128]{2,1,0:T(2,128)(2,1)S(1)}, bf16[512,2,128]{2,1,0:T(2,128)(2,1)}, u32[]{:S(2)}) copy-start(bf16[512,2,128]{2,1,0:T(2,128)(2,1)} %param.29) | copy-start | bytes 786436
  2.7 11.6 %copy-start.6 = (f32[512,512]{1,0:T(8,128)S(1)}, f32[512,512]{1,0:T(8,128)}, u32[]{:S(2)}) copy-start(f32[512,512]{1,0:T(8,128)} %param.24) | copy-start | bytes 3145732
  2.7 22.1 %all-to-all-start = ((bf16[8,64,1024]{2,1,0:T(8,128)(2,1)}), bf16[8,64,1024]{2,1,0:T(8,128)(2,1)S(1)}, u32[]{:S(2)}, u32[]{:S(2)}) async-start(bf16[8,64,1024]{2,1,0:T(8,128)(2,1)} %broadcast_in_dim.14), calls=%async_computation | async-start | bytes 2097152 | tf_op jit(solution)/shard_map/all_to_all | solution.py:257
  10.0 4.3 %copy-start.2 = (f32[512,512]{1,0:T(8,128)S(1)}, f32[512,512]{1,0:T(8,128)}, u32[]{:S(2)}) copy-start(f32[512,512]{1,0:T(8,128)} %param.30) | copy-start | bytes 3145732
  10.0 4.3 %copy-start.3 = (f32[512,512]{1,0:T(8,128)S(1)}, f32[512,512]{1,0:T(8,128)}, u32[]{:S(2)}) copy-start(f32[512,512]{1,0:T(8,128)} %param.31) | copy-start | bytes 3145732
  10.0 4.3 %copy-start.4 = (f32[512,512]{1,0:T(8,128)S(1)}, f32[512,512]{1,0:T(8,128)}, u32[]{:S(2)}) copy-start(f32[512,512]{1,0:T(8,128)} %param.32) | copy-start | bytes 3145732
  10.0 4.3 %copy-start.5 = (f32[512,512]{1,0:T(8,128)S(1)}, f32[512,512]{1,0:T(8,128)}, u32[]{:S(2)}) copy-start(f32[512,512]{1,0:T(8,128)} %param.22) | copy-start | bytes 3145732
  19.8 0.7 copy-start.9
  19.8 6.3 %copy-start.10 = (s32[32]{0:T(128)S(1)}, s32[32]{0:T(128)}, u32[]{:S(2)}) copy-start(s32[32]{0:T(128)} %param.21) | copy-start | bytes 388
  19.8 8.1 %collective-permute-start.1 = (bf16[512,768]{1,0:T(8,128)(2,1)S(1)}, bf16[512,768]{1,0:T(8,128)(2,1)}, u32[]{:S(2)}, u32[]{:S(2)}) collective-permute-start(bf16[512,768]{1,0:T(8,128)(2,1)S(1)} %pad_maximum_fusion.w_ref), channel_id=1, source_target_pairs={{0,8},{1,9},{2,10},{3,11},{4,12},{5,13},{6,14},{7,15},{8,0},{9,1},... | collective-permute-start | bytes 2359304 | tf_op jit(solution)/shard_map/ppermute | solution.py:53
  19.9 8.0 %collective-permute-start.2 = (bf16[512,512]{1,0:T(8,128)(2,1)S(1)}, bf16[512,512]{1,0:T(8,128)(2,1)S(1)}, u32[]{:S(2)}, u32[]{:S(2)}) collective-permute-start(bf16[512,512]{1,0:T(8,128)(2,1)S(1)} %get-tuple-element.13.own_ref), channel_id=1, source_target_pairs={{0,8},{1,9},{2,10},{3,11},{4,12},{5,13},{6,14},{7,15},{8,0},{9,1},... | collective-permute-start | bytes 1572872 | tf_op jit(solution)/shard_map/ppermute | solution.py:53
  26.1 2.3 %collective-permute-start = (bf16[256,1024]{1,0:T(8,128)(2,1)}, bf16[256,1024]{1,0:T(8,128)(2,1)}, u32[]{:S(2)}, u32[]{:S(2)}) collective-permute-start(bf16[256,1024]{1,0:T(8,128)(2,1)} %shard_map.241), channel_id=1, source_target_pairs={{0,8},{1,9},{2,10},{3,11},{4,12},{5,13},{6,14},{7,15},{8,0},{9,1},... | collective-permute-start | bytes 1572872 | tf_op jit(solution)/shard_map/ppermute | solution.py:53
  26.8 21.9 %copy-start.1 = (bf16[32,1,384,128]{3,2,1,0:T(8,128)(2,1)S(1)}, bf16[32,1,384,128]{3,2,1,0:T(8,128)(2,1)}, u32[]{:S(2)}) copy-start(bf16[32,1,384,128]{3,2,1,0:T(8,128)(2,1)} %param.20) | copy-start | bytes 9437188
  28.3 20.4 %copy-start = (bf16[32,1,384,128]{3,2,1,0:T(8,128)(2,1)S(1)}, bf16[32,1,384,128]{3,2,1,0:T(8,128)(2,1)}, u32[]{:S(2)}) copy-start(bf16[32,1,384,128]{3,2,1,0:T(8,128)(2,1)} %param.19) | copy-start | bytes 9437188
  82.3 10.9 %collective-permute-start.3 = (bf16[64,1024]{1,0:T(8,128)(2,1)S(1)}, bf16[64,1024]{1,0:T(8,128)(2,1)S(1)}, u32[]{:S(2)}, u32[]{:S(2)}) collective-permute-start(bf16[64,1024]{1,0:T(8,128)(2,1)S(1)} %reduce_sum.12), channel_id=1, source_target_pairs={{0,0},{1,16},{2,32},{3,48},{4,64},{5,80},{6,96},{7,112},{8,8},{9,2... | collective-permute-start | bytes 393224 | tf_op jit(solution)/shard_map/ppermute | solution.py:53

commit v4 on v3

--- a/solution.py
+++ b/solution.py
@@ -269,28 +269,6 @@
         ],
         axis=1,
     )
-    w_own, w_output = lax.optimization_barrier((w_own, w_output))
-    w_sibling = to_sibling(w_own)
-    w_output_sibling = to_sibling(w_output)
-
-    by_core = slot_rows.reshape(8, 2, SLOTS).transpose(1, 0, 2).reshape(2, 256, 1)
-    mine = lax.dynamic_index_in_dim(by_core, core, 0, False)
-    others = lax.dynamic_index_in_dim(by_core, 1 - core, 0, False)
-    x_send = pl.pallas_call(
-        order_kernel,
-        out_shape=jax.ShapeDtypeStruct((256, 1024), jnp.bfloat16),
-        in_specs=[VMEM] * 2,
-        out_specs=VMEM,
-        compiler_params=params(16),
-    )(others, x_all)
-    x_sibling = to_sibling(x_send)
-    own = pl.pallas_call(
-        own_kernel,
-        out_shape=jax.ShapeDtypeStruct((STEPS, 256, 768), jnp.float32),
-        in_specs=[VMEM] * 3,
-        out_specs=VMEM,
-        compiler_params=params(16),
-    )(mine, x_all, w_own)
     positions = (
         jnp.arange(STEPS, dtype=jnp.int32)[:, None] + lengths[None, :]
     ).reshape(STEPS * SLOTS, 1)
@@ -301,6 +279,30 @@
     cosine = jnp.concatenate([cosine, cosine], axis=1)
     sine = jnp.concatenate([-sine, sine], axis=1)
     length_rows = jnp.repeat(lengths, ROWS)[:, None]
+    by_core = slot_rows.reshape(8, 2, SLOTS).transpose(1, 0, 2).reshape(2, 256, 1)
+    mine = lax.dynamic_index_in_dim(by_core, core, 0, False)
+    others = lax.dynamic_index_in_dim(by_core, 1 - core, 0, False)
+    w_own, w_output, cosine, sine, length_rows, mine, others = lax.optimization_barrier(
+        (w_own, w_output, cosine, sine, length_rows, mine, others)
+    )
+    w_sibling = to_sibling(w_own)
+    w_output_sibling = to_sibling(w_output)
+
+    x_send = pl.pallas_call(
+        order_kernel,
+        out_shape=jax.ShapeDtypeStruct((256, 1024), jnp.bfloat16),
+        in_specs=[VMEM] * 2,
+        out_specs=VMEM,
+        compiler_params=params(16),
+    )(others, x_all)
+    x_sibling = to_sibling(x_send)
+    own = pl.pallas_call(
+        own_kernel,
+        out_shape=jax.ShapeDtypeStruct((STEPS, 256, 768), jnp.float32),
+        in_specs=[VMEM] * 3,
+        out_specs=VMEM,
+        compiler_params=params(16),
+    )(mine, x_all, w_own)
     parts = pl.pallas_call(
         add_kernel,
         out_shape=jax.ShapeDtypeStruct((8, STEPS * SLOTS, 768), jnp.bfloat16),

time: 94.2 us -> 94.1 us (level)
  waiting for transfers between devices: 10.7 us -> 9.59 us
  other arithmetic: 10.2 us -> 11.2 us
    all_to_all x1, waiting for transfers between devices: 4.02 us -> 2.46 us  [per_device(): lax.all_to_all(jnp.broadcast_to(x_own[None], (8, 64, 1024)), TP, 0, 0, ti...]
    convert_element_type x1, other arithmetic: 5.41 us -> 6.66 us  [per_device(): w_output = state_output[0].astype(jnp.bfloat16)]
  transfers between devices with their start and end apart: 5 -> 5, of which waited for: 3 -> 3; matrix products, arithmetic and copies ran while one was open for 11% -> 13% of each run, Pallas kernels for 3% -> 3%
where the time goes in v4:
time: 94.1 us; the launch traced here: 93.7 us
  blocking collectives  49.1 us (52%)
  starting transfers between devices  12.3 us (13%)
  other arithmetic  11.2 us (12%)
  waiting for transfers between devices  9.59 us (10%)
  Pallas kernels  7.01 us (7%)
  local copies, waits for them, and re-layouts  3.64 us (4%)
    all_to_all x1, blocking collectives, per_device(): partial_out = lax.all_to_all(partial_out, TP, 0, 0, tiled=True)  18.6 us
    all_to_all x1, blocking collectives, per_device(): parts = lax.all_to_all(parts, CHIPS, 0, 0, tiled=True)  18.3 us
    all_to_all x1, blocking collectives, per_device(): lax.all_to_all(attended, CHIPS, 0, 0, tiled=True).reshape(512, 512)  12.1 us
    all_to_all x1, starting transfers between devices, per_device(): lax.all_to_all(jnp.broadcast_to(x_own[None], (8, 64, 1024)), TP, 0, 0, ti...  7.15 us
    ppermute x4, waiting for transfers between devices, move(): return lax.ppermute(array, AXES, pairs)  7.13 us
    convert_element_type x1, other arithmetic, per_device(): w_output = state_output[0].astype(jnp.bfloat16)  6.66 us
    ppermute x4, starting transfers between devices, move(): return lax.ppermute(array, AXES, pairs)  5.17 us
    convert_element_type x1, other arithmetic, per_device(): state_keyval[0].astype(jnp.bfloat16).reshape(512, 256)  4.03 us
  transfers between devices with their start and end apart: 5, of which 3 were waited for; matrix products, arithmetic and copies ran while one was open for 13% of the time, Pallas kernels for 3%

profile of v4, /device:TPU:24, one launch (start us, length us, event | category | flops | bytes accessed | tf_op | source)
XLA Modules:
  0.0 93.7 jit_solution(4337619892371451509)
XLA Ops:
  0.6 0.9 copy.35
  1.6 1.1 %broadcast_in_dim.15 = bf16[8,64,1024]{2,1,0:T(8,128)(2,1)} broadcast(bf16[64,1024]{1,0:T(8,128)(2,1)S(1)} %bitcast.23), dimensions={1,2} | broadcast | bytes 1179648 | tf_op jit(solution)/shard_map/broadcast_in_dim | solution.py:258
  2.7 7.2 %all-to-all-start = ((bf16[8,64,1024]{2,1,0:T(8,128)(2,1)}), bf16[8,64,1024]{2,1,0:T(8,128)(2,1)S(1)}, u32[]{:S(2)}, u32[]{:S(2)}) async-start(bf16[8,64,1024]{2,1,0:T(8,128)(2,1)} %broadcast_in_dim.15), calls=%async_computation | async-start | bytes 2097152 | tf_op jit(solution)/shard_map/all_to_all | solution.py:257
  9.9 4.0 %fusion.13 = (bf16[512,2,128]{2,1,0:T(2,128)(2,1)S(1)}, f32[512,2,128]{2,1,0:T(2,128)}, f32[512,2,128]{2,1,0:T(2,128)}, f32[512,2,128]{2,1,0:T(2,128)}) fusion(f32[512,2,128]{2,1,0:T(2,128)S(1)} %copy-done.3, bf16[512,2,128]{2,1,0:T(2,128)(2,1)S(1)} %copy-done.5, f32[512,2,128]{2,1,0:T(2,128)S(1)} %copy-done.4, f32[512,2,128]{2,1,0:T(2,128)} %param.28), kind=kLoop, calls=%fused_computation.28 | loop fusion | flops 2228224 | bytes 3670016 | tf_op jit(solution)/shard_map/convert_element_type | solution.py:268
  14.4 0.2 fusion.6
  14.8 6.7 %fusion.7 = (bf16[512,512]{1,0:T(8,128)(2,1)S(1)}, f32[512,512]{1,0:T(8,128)}, f32[512,512]{1,0:T(8,128)}, f32[512,512]{1,0:T(8,128)}, bf16[512,512]{1,0:T(8,128...) fusion(f32[512,512]{1,0:T(8,128)S(1)} %copy-done.2, bf16[512,512]{1,0:T(8,128)(2,1)} %param.33, ...), kind=kLoop, calls=%fused_computation.26 | loop fusion | flops 8912896 | bytes 14680064 | tf_op jit(solution)/shard_map/convert_element_type | solution.py:262
  21.6 0.5 collective-permute-start.2
  22.1 0.1 copy.31.slots_ref
  22.2 2.5 %all-to-all-done = bf16[8,64,1024]{2,1,0:T(8,128)(2,1)S(1)} async-done(((bf16[8,64,1024]{2,1,0:T(8,128)(2,1)}), bf16[8,64,1024]{2,1,0:T(8,128)(2,1)S(1)}, u32[]{:S(2)}, u32[]{:S(2)}) %all-to-all-start) | async-done | bytes 1048608 | tf_op jit(solution)/shard_map/all_to_all | solution.py:257
  24.7 1.3 %shard_map.241 = bf16[256,1024]{1,0:T(8,128)(2,1)} custom-call(s32[256,1]{1,0:T(8,128)S(1)} %copy.31.slots_ref, bf16[512,1024]{1,0:T(8,128)(2,1)S(1)} %bitcast.16), custom_call_target="tpu_custom_call" | custom-call | tf_op jit(solution)/shard_map/pallas_call | solution.py:291
  26.0 0.1 copy.30.slots_ref
  26.1 0.1 copy.32.len_ref
  26.3 1.1 %shard_map.240.own_ref = f32[2,256,768]{2,1,0:T(8,128)S(1)} custom-call(s32[256,1]{1,0:T(8,128)S(1)} %copy.30.slots_ref, bf16[512,1024]{1,0:T(8,128)(2,1)S(1)} %bitcast.17, bf16[512,768]{1,0:T(8,128)(2,1)S(1)} %pad_maximum_fusion.w_ref), custom_call_target="tpu_custom_call" | custom-call | tf_op jit(solution)/shard_map/pallas_call | solution.py:299
  27.4 0.8 collective-permute-done.x_ref
  28.2 2.0 %shard_map.242 = bf16[8,64,768]{2,1,0:T(8,128)(2,1)S(1)} custom-call(f32[2,256,768]{2,1,0:T(8,128)S(1)} %shard_map.240.own_ref, bf16[256,1024]{1,0:T(8,128)(2,1)} %collective-permute-done.x_ref, bf16[512,768]{1,0:T(8,128)(2,1)} %collective-permute-done.1.w_ref, f32[64,128]{1,0:T(8,128)S(1)} %get-tuple-element.20.cos_ref, ...), custom_call_target="tpu_custom_call" | custom-call | tf_op jit(solution)/shard_map/pallas_call | solution.py:306
  30.2 18.3 %all_to_all.20.parts_ref = bf16[8,64,768]{2,1,0:T(8,128)(2,1)S(1)} all-to-all(bf16[8,64,768]{2,1,0:T(8,128)(2,1)S(1)} %shard_map.242), channel_id=1, replica_groups=mesh['z'=4,'xl'=2,'c'=2,'y'=4,'xh'=2] {'z','xl'}, dimensions={0} | all-to-all | bytes 1572864 | tf_op jit(solution)/shard_map/all_to_all | solution.py:313
  48.6 1.9 %shard_map.243 = bf16[8,64,512]{2,1,0:T(8,128)(2,1)S(1)} custom-call(bf16[8,64,768]{2,1,0:T(8,128)(2,1)S(1)} %all_to_all.20.parts_ref, f32[64,128]{1,0:T(8,128)S(1)} %get-tuple-element.20.cos_ref, f32[64,128]{1,0:T(8,128)S(1)} %get-tuple-element.21.sin_ref, s32[256,1]{1,0:T(8,128)S(1)} %copy.32.len_ref, bf16[32,384,128]{2,1,0:T(8,128)(2,1)S(1)} %bitcast.18, ...), custom_call_target="tpu_custom_call" | custom-call | tf_op jit(solution)/shard_map/pallas_call | solution.py:200
  50.5 12.1 %all_to_all.21 = bf16[8,64,512]{2,1,0:T(8,128)(2,1)S(1)} all-to-all(bf16[8,64,512]{2,1,0:T(8,128)(2,1)S(1)} %shard_map.243), channel_id=1, replica_groups=mesh['z'=4,'xl'=2,'c'=2,'y'=4,'xh'=2] {'z','xl'}, dimensions={0} | all-to-all | bytes 1048576 | tf_op jit(solution)/shard_map/all_to_all | solution.py:323
  62.6 0.7 shard_map.244
  63.3 18.6 %all_to_all.22 = bf16[8,64,1024]{2,1,0:T(8,128)(2,1)S(1)} all-to-all(bf16[8,64,1024]{2,1,0:T(8,128)(2,1)S(1)} %shard_map.244), channel_id=1, replica_groups=mesh['z'=4,'xl'=2,'c'=2,'y'=4,'xh'=2] {'y','xh'}, dimensions={0} | all-to-all | bytes 2097152 | tf_op jit(solution)/shard_map/all_to_all | solution.py:325
  82.0 0.2 reduce_sum.12
  82.2 4.6 %collective-permute-start.3 = (bf16[64,1024]{1,0:T(8,128)(2,1)S(1)}, bf16[64,1024]{1,0:T(8,128)(2,1)S(1)}, u32[]{:S(2)}, u32[]{:S(2)}) collective-permute-start(bf16[64,1024]{1,0:T(8,128)(2,1)S(1)} %reduce_sum.12), channel_id=1, source_target_pairs={{0,0},{1,16},{2,32},{3,48},{4,64},{5,80},{6,96},{7,112},{8,8},{9,2... | collective-permute-start | bytes 393224 | tf_op jit(solution)/shard_map/ppermute | solution.py:53
  86.8 6.3 %collective-permute-done.3 = bf16[64,1024]{1,0:T(8,128)(2,1)S(1)} collective-permute-done((bf16[64,1024]{1,0:T(8,128)(2,1)S(1)}, bf16[64,1024]{1,0:T(8,128)(2,1)S(1)}, u32[]{:S(2)}, u32[]{:S(2)}) %collective-permute-start.3) | collective-permute-done | bytes 131104 | tf_op jit(solution)/shard_map/ppermute | solution.py:53
  93.0 0.7 reshape.79
  (32 shorter events, 0.8 us)
Async XLA Ops:
  1.6 8.3 %copy-start.3 = (f32[512,2,128]{2,1,0:T(2,128)S(1)}, f32[512,2,128]{2,1,0:T(2,128)}, u32[]{:S(2)}) copy-start(f32[512,2,128]{2,1,0:T(2,128)} %param.26) | copy-start | bytes 1572868
  1.6 8.3 %copy-start.4 = (f32[512,2,128]{2,1,0:T(2,128)S(1)}, f32[512,2,128]{2,1,0:T(2,128)}, u32[]{:S(2)}) copy-start(f32[512,2,128]{2,1,0:T(2,128)} %param.27) | copy-start | bytes 1572868
  1.6 8.3 %copy-start.5 = (bf16[512,2,128]{2,1,0:T(2,128)(2,1)S(1)}, bf16[512,2,128]{2,1,0:T(2,128)(2,1)}, u32[]{:S(2)}) copy-start(bf16[512,2,128]{2,1,0:T(2,128)(2,1)} %param.29) | copy-start | bytes 786436
  2.7 22.0 %all-to-all-start = ((bf16[8,64,1024]{2,1,0:T(8,128)(2,1)}), bf16[8,64,1024]{2,1,0:T(8,128)(2,1)S(1)}, u32[]{:S(2)}, u32[]{:S(2)}) async-start(bf16[8,64,1024]{2,1,0:T(8,128)(2,1)} %broadcast_in_dim.15), calls=%async_computation | async-start | bytes 2097152 | tf_op jit(solution)/shard_map/all_to_all | solution.py:257
  9.9 4.1 %copy-start.7 = (s32[32]{0:T(128)S(1)}, s32[32]{0:T(128)}, u32[]{:S(2)}) copy-start(s32[32]{0:T(128)} %param.21) | copy-start | bytes 388
  9.9 4.4 %copy-start.6 = (s32[512]{0:T(512)S(1)}, s32[512]{0:T(512)}, u32[]{:S(2)}) copy-start(s32[512]{0:T(512)} %param.18) | copy-start | bytes 6148
  9.9 4.8 %copy-start.2 = (f32[512,512]{1,0:T(8,128)S(1)}, f32[512,512]{1,0:T(8,128)}, u32[]{:S(2)}) copy-start(f32[512,512]{1,0:T(8,128)} %param.30) | copy-start | bytes 3145732
  21.5 5.9 %collective-permute-start.1 = (bf16[512,768]{1,0:T(8,128)(2,1)S(1)}, bf16[512,768]{1,0:T(8,128)(2,1)}, u32[]{:S(2)}, u32[]{:S(2)}) collective-permute-start(bf16[512,768]{1,0:T(8,128)(2,1)S(1)} %pad_maximum_fusion.w_ref), channel_id=1, source_target_pairs={{0,8},{1,9},{2,10},{3,11},{4,12},{5,13},{6,14},{7,15},{8,0},{9,1},... | collective-permute-start | bytes 2359304 | tf_op jit(solution)/shard_map/ppermute | solution.py:53
  21.6 5.8 %collective-permute-start.2 = (bf16[512,512]{1,0:T(8,128)(2,1)S(1)}, bf16[512,512]{1,0:T(8,128)(2,1)S(1)}, u32[]{:S(2)}, u32[]{:S(2)}) collective-permute-start(bf16[512,512]{1,0:T(8,128)(2,1)S(1)} %get-tuple-element.23.own_ref), channel_id=1, source_target_pairs={{0,8},{1,9},{2,10},{3,11},{4,12},{5,13},{6,14},{7,15},{8,0},{9,1},... | collective-permute-start | bytes 1572872 | tf_op jit(solution)/shard_map/ppermute | solution.py:53
  26.0 2.3 %collective-permute-start = (bf16[256,1024]{1,0:T(8,128)(2,1)}, bf16[256,1024]{1,0:T(8,128)(2,1)}, u32[]{:S(2)}, u32[]{:S(2)}) collective-permute-start(bf16[256,1024]{1,0:T(8,128)(2,1)} %shard_map.241), channel_id=1, source_target_pairs={{0,8},{1,9},{2,10},{3,11},{4,12},{5,13},{6,14},{7,15},{8,0},{9,1},... | collective-permute-start | bytes 1572872 | tf_op jit(solution)/shard_map/ppermute | solution.py:53
  26.3 22.3 %copy-start.1 = (bf16[32,1,384,128]{3,2,1,0:T(8,128)(2,1)S(1)}, bf16[32,1,384,128]{3,2,1,0:T(8,128)(2,1)}, u32[]{:S(2)}) copy-start(bf16[32,1,384,128]{3,2,1,0:T(8,128)(2,1)} %param.20) | copy-start | bytes 9437188
  28.2 20.4 %copy-start = (bf16[32,1,384,128]{3,2,1,0:T(8,128)(2,1)S(1)}, bf16[32,1,384,128]{3,2,1,0:T(8,128)(2,1)}, u32[]{:S(2)}) copy-start(bf16[32,1,384,128]{3,2,1,0:T(8,128)(2,1)} %param.19) | copy-start | bytes 9437188
  82.2 10.9 %collective-permute-start.3 = (bf16[64,1024]{1,0:T(8,128)(2,1)S(1)}, bf16[64,1024]{1,0:T(8,128)(2,1)S(1)}, u32[]{:S(2)}, u32[]{:S(2)}) collective-permute-start(bf16[64,1024]{1,0:T(8,128)(2,1)S(1)} %reduce_sum.12), channel_id=1, source_target_pairs={{0,0},{1,16},{2,32},{3,48},{4,64},{5,80},{6,96},{7,112},{8,8},{9,2... | collective-permute-start | bytes 393224 | tf_op jit(solution)/shard_map/ppermute | solution.py:53
